TPU v7x, 256 devices: a whole 4x4x8 slice. The times are simulated.
256 devices in a mesh: gx: 8 (over z_lo, x), gy: 8 (over y, core), gz: 4 (over z_hi).
Axes of the slice: x: 4, y: 4, z: 8 (z_hi: 4, z_lo: 2; z = z_hi * 2 + z_lo), core: 2. Of those that a mesh axis runs over, the one named last changes fastest.
Arguments:
- displacements: float32 [3, 16, 16, 128], P(None, 'gx', 'gy', 'gz'), may hold values from -0.3 to 0.3
- species: int32 [16, 16, 128], P('gx', 'gy', 'gz'), may hold values from 0 to 2
- neighbor_index: int32 [32, 16, 16, 128], P(None, 'gx', 'gy', 'gz'), may hold values from 0 to 543, as said below
- probes: float32 [8, 3, 16, 16, 128], P(None, None, 'gx', 'gy', 'gz'), may hold values from -4 to 4
- embedding: float32 [3, 128], replicated, may hold values from -5 to 5
- w_radial1: float32 [8, 64], replicated, may hold values from -2 to 2
- w_radial2: float32 [64, 128], replicated, may hold values from -0.75 to 0.75
- w_node: float32 [128, 128], replicated, may hold values from -0.5 to 0.5
- readout: float32 [128], replicated, may hold values from -0.5 to 0.5
- spectral_radius: float32 [1], replicated, may hold values from 0.15 to 0.4
Outputs:
- chebyshev: float32 [2, 8, 3, 16, 16, 128], P(None, None, None, 'gx', 'gy', 'gz')
- moments: float32 [4, 8], replicated
Inputs may be any that keep to these rules, and one draw needn't show every extreme that they name: `neighbor_index`: entry n of atom a is the row-major flat index, in a block of (4) x (4) x (34) sites formed by a's domain and one layer of adjacent sites around it, either of a lattice site adjacent to a (differing by -1, 0 or 1 in each coordinate, not a itself) or of a itself for an empty slot; no adjacent site appears twice in one list.
All inputs are finite; a program needn't handle non-finite values.
Results may differ from a plain program's by a relative error of at most 0.0003.
Values sent between devices are 32-bit elements; how exact they have to be, the bound alone decides.
A program may use at most 192 MiB of HBM per device.

v0:
```python
import math

import jax
import jax.numpy as jnp
from jax import lax
from jax.sharding import PartitionSpec as P

STEPS = 3


SPACING = 2.2
CUTOFF = 5.0
NORM_SCALE = 0.22360679774997896
MASSES = (28.0855, 15.999, 22.99)
HIGHEST = lax.Precision.HIGHEST
OFFSET_CODES = tuple((code for code in range(27) if code != 13))


def padded_2(cells, sides, width):
    for axis, dim in sides:
        count = lax.axis_size(axis)
        head = lax.slice_in_dim(cells, 0, width, axis=dim)
        tail = lax.slice_in_dim(cells, cells.shape[dim] - width, cells.shape[dim], axis=dim)
        cells = jnp.concatenate(
            [
                lax.ppermute(tail, axis, [(i, (i + 1) % count) for i in range(count)]),
                cells,
                lax.ppermute(head, axis, [((i + 1) % count, i) for i in range(count)]),
            ],
            axis=dim,
        )
    return cells


def from_behind(value, axis, by):
    size = lax.axis_size(axis)
    return lax.ppermute(value, axis, [(i, (i + by) % size) for i in range(size)])


def species_rows(species_ids, lookup_table):
    onehot = (species_ids[..., None] == jnp.arange(lookup_table.shape[0], dtype=jnp.int32)).astype(
        jnp.float32
    )
    return jnp.dot(onehot, lookup_table, precision=HIGHEST)


def radial_terms(distance, filled, w_radial1, w_radial2):

    def radial(radius_in):
        frequency = jnp.arange(1, w_radial1.shape[0] + 1).astype(jnp.float32) * (math.pi / CUTOFF)
        bessel = (
            math.sqrt(2.0 / CUTOFF)
            * jnp.sin(radius_in[..., None] * frequency)
            / radius_in[..., None]
        )
        scaled = radius_in / CUTOFF
        envelope = jnp.where(filled, (1.0 - scaled * scaled) ** 2, 0.0)
        hidden = jax.nn.silu(jnp.dot(bessel, w_radial1, precision=HIGHEST))
        return jnp.dot(hidden, w_radial2, precision=HIGHEST) * envelope[..., None]

    unit_tangent = jnp.ones_like(distance)

    def slope(radius_in):
        return jax.jvp(radial, (radius_in,), (unit_tangent,))

    (radial_value, first_order), (unused, second_order) = jax.jvp(
        slope, (distance,), (unit_tangent,)
    )
    return (radial_value, first_order, second_order)


def shift_view(field, code):
    step_x = code // 9 - 1
    step_y = code // 3 % 3 - 1
    step_z = code % 3 - 1
    size_x, size_y, size_z = field.shape[-3:]
    return field[
        ...,
        1 + step_x : size_x - 1 + step_x,
        1 + step_y : size_y - 1 + step_y,
        1 + step_z : size_z - 1 + step_z,
    ]


def all_views(field):
    return jnp.stack([shift_view(field, code) for code in OFFSET_CODES], 0)


def edge_lengths(positions, present, lattice):
    centre = shift_view(positions, 13)
    edge_vec = lattice[:, :, None, None, None] + all_views(positions) - centre[None]
    squared = jnp.sum(edge_vec * edge_vec, 1)
    return jnp.sqrt(jnp.where(present, squared, 1.0)).reshape(len(OFFSET_CODES), -1)


def local_codes(neighbor_index):
    depth_y = neighbor_index.shape[2] + 2
    depth_z = neighbor_index.shape[3] + 2
    along_x = neighbor_index // (depth_y * depth_z)
    along_y = neighbor_index // depth_z % depth_y
    along_z = neighbor_index % depth_z
    grid_x = lax.broadcasted_iota(jnp.int32, neighbor_index.shape, 1) + 1
    grid_y = lax.broadcasted_iota(jnp.int32, neighbor_index.shape, 2) + 1
    grid_z = lax.broadcasted_iota(jnp.int32, neighbor_index.shape, 3) + 1
    return (along_x - grid_x + 1) * 9 + (along_y - grid_y + 1) * 3 + (along_z - grid_z + 1)


def fold_dim(gradient, along_dim, sender):
    extent = gradient.shape[along_dim]
    lower_rim = lax.slice_in_dim(gradient, 0, 1, axis=along_dim)
    upper_rim = lax.slice_in_dim(gradient, extent - 1, extent, axis=along_dim)
    interior = lax.slice_in_dim(gradient, 1, extent - 1, axis=along_dim)
    for direction, payload, target in ((-1, lower_rim, extent - 3), (1, upper_rim, 0)):
        arrived = sender(payload, direction)
        selector = [slice(None)] * interior.ndim
        selector[along_dim] = slice(target, target + 1)
        interior = interior.at[tuple(selector)].add(arrived)
    return interior


def on_device(
    displacements,
    species,
    neighbor_index,
    probes,
    embedding,
    w_radial1,
    w_radial2,
    w_node,
    readout,
    spectral_radius,
):
    probe_count = probes.shape[0]
    channels = embedding.shape[1]
    offset_codes = local_codes(neighbor_index)
    static = jnp.concatenate([displacements, species.astype(jnp.float32)[None]], 0)
    masses = species_rows(species, jnp.array(MASSES, dtype=jnp.float32)[:, None])[..., 0]
    inv_root = 1.0 / jnp.sqrt(masses)
    frame_data = padded_2(static, (("gx", 1), ("gy", 2), ("gz", 3)), 1)
    frame_dims = tuple(frame_data.shape[1:])
    frame_offset = frame_data[:3]
    frame_species = frame_data[3].astype(jnp.int32)
    code_values = jnp.array(OFFSET_CODES, dtype=jnp.int32)
    present = jnp.any(offset_codes[None] == code_values[:, None, None, None, None], axis=1)
    lattice = (
        jnp.array(
            [[code // 9 - 1, code // 3 % 3 - 1, code % 3 - 1] for code in OFFSET_CODES],
            dtype=jnp.float32,
        )
        * SPACING
    )
    base_distance = edge_lengths(frame_offset, present, lattice)
    filled_rows = present.reshape(len(OFFSET_CODES), -1)
    neighbour_species = all_views(frame_species).reshape(len(OFFSET_CODES), -1)
    centre_count = filled_rows.shape[1]

    def code_tables(running, code_item):
        distance_row, filled_row, species_row = code_item
        radial_value, first_order, second_order = radial_terms(
            distance_row, filled_row, w_radial1, w_radial2
        )
        neighbour_rows = species_rows(species_row, embedding) * NORM_SCALE
        return (
            running + radial_value * neighbour_rows,
            (first_order * neighbour_rows, second_order * neighbour_rows),
        )

    message_base, (first_table, second_table) = lax.scan(
        code_tables,
        jnp.zeros((centre_count, channels), jnp.float32),
        (base_distance, filled_rows, neighbour_species),
    )
    centre_rows = species_rows(shift_view(frame_species, 13).reshape(-1), embedding)

    def energy(positions):
        change = edge_lengths(positions, present, lattice) - base_distance
        message = message_base + jnp.einsum("nc,nck->ck", change, first_table, precision=HIGHEST)
        message = message + 0.5 * jnp.einsum(
            "nc,nck->ck", change * change, second_table, precision=HIGHEST
        )
        node_feat = jax.nn.silu(jnp.dot(message, w_node, precision=HIGHEST) + centre_rows)
        return jnp.sum(jnp.dot(node_feat, readout, precision=HIGHEST))

    force_field = jax.grad(energy)

    def hessian(tangents):
        return jax.vmap(lambda vector: jax.jvp(force_field, (frame_offset,), (vector,))[1])(
            tangents
        )

    def operate(vectors):
        scaled = (vectors * inv_root).reshape((probe_count * 3,) + vectors.shape[2:])
        padded = padded_2(scaled, (("gx", 1), ("gy", 2), ("gz", 3)), 1)
        product = hessian(padded.reshape((probe_count, 3) + frame_dims)).reshape(
            (probe_count * 3,) + frame_dims
        )
        product = fold_dim(
            product, 3, lambda payload, direction: from_behind(payload, "gz", direction)
        )
        product = fold_dim(
            product, 2, lambda payload, direction: from_behind(payload, "gy", direction)
        )
        product = fold_dim(
            product, 1, lambda payload, direction: from_behind(payload, "gx", direction)
        )
        return product.reshape(probes.shape) * inv_root / spectral_radius[0]

    def record(vector):
        local_term = jnp.sum(probes * vector, axis=(1, 2, 3, 4))
        return lax.psum(local_term, ("gx", "gy", "gz"))

    previous = probes
    partials = [record(probes)]
    current = operate(probes)
    partials.append(record(current))
    for iteration in range(2, STEPS + 1):
        following = 2.0 * operate(current) - previous
        previous, current = (current, following)
        partials.append(record(current))
    stacked = jnp.stack(partials)
    return (jnp.stack([previous, current]), stacked)


def solution(mesh):
    placed = (
        P(None, "gx", "gy", "gz"),
        P("gx", "gy", "gz"),
        P(None, "gx", "gy", "gz"),
        P(None, None, "gx", "gy", "gz"),
        P(),
        P(),
        P(),
        P(),
        P(),
        P(),
    )
    return jax.shard_map(
        on_device,
        mesh=mesh,
        in_specs=placed,
        out_specs=(P(None, None, None, "gx", "gy", "gz"), P()),
        check_vma=False,
    )
```

profile of v0, /device:TPU:1, one launch (start us, length us, event | category | flops | bytes accessed | tf_op | source)
XLA Modules:
  0.0 556.6 jit_solution(11854463581249655253)
XLA Ops:
  8.8 3.6 collective-permute-start.1
  21.1 3.0 collective-permute-start.10
  24.2 3.1 collective-permute-start.11
  33.9 170.6 %while.38 = (s32[]{:T(128)}, f32[128,128]{1,0:T(8,128)S(1)}, f32[26,128,128]{2,0,1:T(8,128)S(1)}, f32[26,128,128]{2,0,1:T(8,128)}, f32[26,128]{1,0:T(8,128)S(1)}...) while((s32[]{:T(128)}, f32[128,128]{1,0:T(8,128)S(1)}, ...), condition=%wide.region_3.4_spmd.clone, body=%wide.region_2.3_spmd.clone.sunk | while | flops 41247000 | bytes 1461139 | solution.py:168
  36.2 3.0 dynamic_update_slice.26
  42.7 3.0 dynamic_update_slice.26
  49.3 3.0 dynamic_update_slice.26
  55.8 3.0 dynamic_update_slice.26
  62.4 3.0 dynamic_update_slice.26
  68.9 3.0 dynamic_update_slice.26
  75.5 3.0 dynamic_update_slice.26
  82.0 3.0 dynamic_update_slice.26
  88.6 2.9 dynamic_update_slice.26
  95.1 2.9 dynamic_update_slice.26
  101.6 2.9 dynamic_update_slice.26
  108.2 2.9 dynamic_update_slice.26
  114.7 2.9 dynamic_update_slice.26
  121.2 2.9 dynamic_update_slice.26
  127.8 2.9 dynamic_update_slice.26
  134.3 2.9 dynamic_update_slice.26
  140.8 3.0 dynamic_update_slice.26
  147.4 3.0 dynamic_update_slice.26
  154.0 3.0 dynamic_update_slice.26
  160.6 3.0 dynamic_update_slice.26
  167.1 3.0 dynamic_update_slice.26
  173.7 3.0 dynamic_update_slice.26
  180.3 3.0 dynamic_update_slice.26
  186.9 3.0 dynamic_update_slice.26
  193.4 3.0 dynamic_update_slice.26
  200.0 3.0 dynamic_update_slice.26
  209.5 3.4 fusion.252
  212.9 3.4 fusion.251
  221.5 4.1 collective-permute-start.4
  226.4 3.3 collective-permute-done.4
  243.8 3.9 convolution_bitcast_fusion.4
  247.6 3.5 fusion.83
  257.3 3.0 collective-permute-start.12
  264.5 8.8 %scatter-add.60 = f32[24,4,4,32]{3,2,1,0:T(4,128)S(1)} dynamic-update-slice(f32[24,4,4,32]{3,2,1,0:T(4,128)S(1)} %slice.1528, f32[24,4,4,1]{3,2,1,0:T(4,128)S(1)} %slice_add_fusion.5, s32[]{:T(128)} %constant.600.clone.1, s32[]{:T(128)} %constant.600.clone.1, s32[]{:T(128)} %constant.600.clone.1, s32[]{:T(128)} %constant.611.clone.1) | dynamic-update-slice | bytes 3076 | tf_op jit(solution)/shard_map/scatter-add | solution.py:117
  275.9 6.5 %collective-permute-start.14 = (f32[24,4,1,32]{3,2,1,0:T(1,128)S(1)}, f32[24,4,1,32]{3,2,1,0:T(1,128)S(1)}, u32[]{:S(2)}, u32[]{:S(2)}) collective-permute-start(f32[24,4,1,32]{3,2,1,0:T(1,128)S(1)} %get-tuple-element.702), channel_id=1, source_target_pairs={{0,28},{4,0},{8,4},{12,8},{16,12},{20,16},{24,20},{28,24},{1,29},{... | collective-permute-start | bytes 36872 | tf_op jit(solution)/shard_map/ppermute | solution.py:37
  282.4 3.0 collective-permute-start.15
  293.9 3.9 collective-permute-done.17
  297.9 3.6 collective-permute-start.19
  309.3 3.6 collective-permute-start.22
  313.1 3.4 collective-permute-done.22
  316.6 5.6 %collective-permute-done.23 = f32[24,4,4,1]{3,2,1,0:T(4,128)S(1)} collective-permute-done((f32[24,4,4,1]{3,2,1,0:T(4,128)S(1)}, f32[24,4,4,1]{3,2,1,0:T(4,128)S(1)}, u32[]{:S(2)}, u32[]{:S(2)}) %collective-permute-start.23) | collective-permute-done | bytes 1568 | tf_op jit(solution)/shard_map/ppermute | solution.py:28
  334.4 3.9 convolution_bitcast_fusion.2
  338.3 3.5 fusion.87
  350.8 4.3 collective-permute-done.24
  355.3 8.8 %scatter-add.70 = f32[24,4,4,32]{3,2,1,0:T(4,128)S(1)} dynamic-update-slice(f32[24,4,4,32]{3,2,1,0:T(4,128)S(1)} %slice.1576, f32[24,4,4,1]{3,2,1,0:T(4,128)S(1)} %slice_add_fusion.3, s32[]{:T(128)} %constant.600.clone.1, s32[]{:T(128)} %constant.600.clone.1, s32[]{:T(128)} %constant.600.clone.1, s32[]{:T(128)} %constant.611.clone.1) | dynamic-update-slice | bytes 3076 | tf_op jit(solution)/shard_map/scatter-add | solution.py:117
  369.1 5.5 collective-permute-start.27
  383.1 3.4 collective-permute-done.29
  387.4 3.6 collective-permute-start.31
  395.0 3.9 collective-permute-start.33
  400.3 4.4 collective-permute-start.35
  404.7 3.1 collective-permute-done.34
  420.8 3.9 convolution_bitcast_fusion
  424.7 3.5 fusion.91
  432.6 5.1 collective-permute-start.36
  438.2 4.3 collective-permute-done.36
  442.6 8.8 %scatter-add.80 = f32[24,4,4,32]{3,2,1,0:T(4,128)S(1)} dynamic-update-slice(f32[24,4,4,32]{3,2,1,0:T(4,128)S(1)} %slice.1624, f32[24,4,4,1]{3,2,1,0:T(4,128)S(1)} %slice_add_fusion.1, s32[]{:T(128)} %constant.600.clone.1, s32[]{:T(128)} %constant.600.clone.1, s32[]{:T(128)} %constant.600.clone.1, s32[]{:T(128)} %constant.611.clone.1) | dynamic-update-slice | bytes 3076 | tf_op jit(solution)/shard_map/scatter-add | solution.py:117
  454.1 6.4 %collective-permute-start.38 = (f32[24,4,1,32]{3,2,1,0:T(1,128)S(1)}, f32[24,4,1,32]{3,2,1,0:T(1,128)S(1)}, u32[]{:S(2)}, u32[]{:S(2)}) collective-permute-start(f32[24,4,1,32]{3,2,1,0:T(1,128)S(1)} %get-tuple-element.690), channel_id=1, source_target_pairs={{0,28},{4,0},{8,4},{12,8},{16,12},{20,16},{24,20},{28,24},{1,29},{... | collective-permute-start | bytes 36872 | tf_op jit(solution)/shard_map/ppermute | solution.py:37
  468.5 5.3 collective-permute-start.40
  474.8 3.9 collective-permute-done.41
  479.8 76.1 %all-reduce.81 = (f32[1,8]{1,0:T(1,128)S(1)}, f32[1,8]{1,0:T(1,128)S(1)}, f32[1,8]{1,0:T(1,128)S(1)}, f32[1,8]{1,0:T(1,128)S(1)}) all-reduce(f32[1,8]{1,0:T(1,128)S(1)} %bitcast.1039, f32[1,8]{1,0:T(1,128)S(1)} %bitcast.1041, f32[1,8]{1,0:T(1,128)S(1)} %bitcast.1038, ...), channel_id=1, replica_groups=mesh['gx'=8,'gy'=8,'gz'=4] {'gx','gy','gz'}, use_global_device_ids=true, to_apply=%region_17.20 | all-reduce | flops 32 | bytes 256 | tf_op jit(solution)/shard_map/psum | solution.py:210
  (755 shorter events, 239.0 us)
Async XLA Ops:
  0.6 207.5 %copy-start = (f32[128,128]{1,0:T(8,128)S(1)}, f32[128,128]{1,0:T(8,128)}, u32[]{:S(2)}) copy-start(f32[128,128]{1,0:T(8,128)} %param.67) | copy-start | bytes 196612
  0.6 30.4 %copy-start.44 = (f32[26,3]{1,0:T(8,128)S(1)}, f32[26,3]{1,0:T(8,128)}, u32[]{:S(2)}) copy-start(f32[26,3]{1,0:T(8,128)} %constant.782) | copy-start | bytes 940
  0.7 29.2 %copy-start.11 = (f32[3,2,2,32]{3,2,1,0:T(2,128)S(1)}, f32[3,2,2,32]{3,2,1,0:T(2,128)}, u32[]{:S(2)}) copy-start(f32[3,2,2,32]{3,2,1,0:T(2,128)} %param.60) | copy-start | bytes 4612
  2.1 11.7 %collective-permute-start.6 = (f32[4,1,2,32]{3,2,1,0:T(2,128)S(1)}, f32[4,1,2,32]{3,2,1,0:T(2,128)S(1)}, u32[]{:S(2)}, u32[]{:S(2)}) collective-permute-start(f32[4,1,2,32]{3,2,1,0:T(2,128)S(1)} %get-tuple-element.766), channel_id=1, source_target_pairs={{0,32},{32,64},{64,96},{96,128},{128,160},{160,192},{192,224},{224... | collective-permute-start | bytes 3080 | tf_op jit(solution)/shard_map/ppermute | solution.py:26
  4.1 9.7 %collective-permute-start.7 = (f32[4,1,2,32]{3,2,1,0:T(2,128)S(1)}, f32[4,1,2,32]{3,2,1,0:T(2,128)S(1)}, u32[]{:S(2)}, u32[]{:S(2)}) collective-permute-start(f32[4,1,2,32]{3,2,1,0:T(2,128)S(1)} %get-tuple-element.767), channel_id=1, source_target_pairs={{32,0},{64,32},{96,64},{128,96},{160,128},{192,160},{224,192},{0,2... | collective-permute-start | bytes 3080 | tf_op jit(solution)/shard_map/ppermute | solution.py:28
  8.7 207.6 %collective-permute-start = (f32[24,1,2,32]{3,2,1,0:T(2,128)S(1)}, f32[24,1,2,32]{3,2,1,0:T(2,128)S(1)}, u32[]{:S(2)}, u32[]{:S(2)}) collective-permute-start(f32[24,1,2,32]{3,2,1,0:T(2,128)S(1)} %get-tuple-element.731), channel_id=1, source_target_pairs={{0,32},{32,64},{64,96},{96,128},{128,160},{160,192},{192,224},{224... | collective-permute-start | bytes 18440 | tf_op jit(solution)/shard_map/ppermute | solution.py:26
  8.8 207.5 %collective-permute-start.1 = (f32[24,1,2,32]{3,2,1,0:T(2,128)S(1)}, f32[24,1,2,32]{3,2,1,0:T(2,128)S(1)}, u32[]{:S(2)}, u32[]{:S(2)}) collective-permute-start(f32[24,1,2,32]{3,2,1,0:T(2,128)S(1)} %get-tuple-element.732), channel_id=1, source_target_pairs={{32,0},{64,32},{96,64},{128,96},{160,128},{192,160},{224,192},{0,2... | collective-permute-start | bytes 18440 | tf_op jit(solution)/shard_map/ppermute | solution.py:28
  13.7 20.1 %copy-start.31 = (f32[3,128]{1,0:T(4,128)S(1)}, f32[3,128]{1,0:T(4,128)}, u32[]{:S(2)}) copy-start(f32[3,128]{1,0:T(4,128)} %param.64) | copy-start | bytes 4612
  13.8 20.1 %copy-start.49 = (f32[64,128]{1,0:T(8,128)S(1)}, f32[64,128]{1,0:T(8,128)}, u32[]{:S(2)}) copy-start(f32[64,128]{1,0:T(8,128)} %param.66) | copy-start | bytes 98308
  13.8 20.1 %copy-start.50 = (f32[8,64]{1,0:T(8,128)S(1)}, f32[8,64]{1,0:T(8,128)}, u32[]{:S(2)}) copy-start(f32[8,64]{1,0:T(8,128)} %param.65) | copy-start | bytes 6148
  14.5 4.5 collective-permute-start.8
  17.3 3.1 collective-permute-start.9
  19.0 14.9 %copy-start.20 = (pred[26,2,2,32]{0,3,2,1:T(8,128)(4,1)}, pred[26,2,2,32]{0,3,2,1:T(8,128)(4,1)S(1)}, u32[]{:S(2)}) copy-start(pred[26,2,2,32]{0,3,2,1:T(8,128)(4,1)S(1)} %copy.132) | copy-start | bytes 9988
  21.1 7.7 %collective-permute-start.10 = (f32[4,4,4,1]{3,2,1,0:T(4,128)S(1)}, f32[4,4,4,1]{3,2,1,0:T(4,128)S(1)}, u32[]{:S(2)}, u32[]{:S(2)}) collective-permute-start(f32[4,4,4,1]{3,2,1,0:T(4,128)S(1)} %get-tuple-element.736), channel_id=1, source_target_pairs={{0,1},{1,2},{2,3},{3,0},{4,5},{5,6},{6,7},{7,4},{8,9},{9,10},{10,1... | collective-permute-start | bytes 776 | tf_op jit(solution)/shard_map/ppermute | solution.py:26
  24.2 5.5 collective-permute-start.11
  216.4 2.6 collective-permute-start.2
  217.6 3.5 collective-permute-start.3
  221.5 8.2 %collective-permute-start.4 = (f32[24,4,4,1]{3,2,1,0:T(4,128)S(1)}, f32[24,4,4,1]{3,2,1,0:T(4,128)S(1)}, u32[]{:S(2)}, u32[]{:S(2)}) collective-permute-start(f32[24,4,4,1]{3,2,1,0:T(4,128)S(1)} %get-tuple-element.705), channel_id=1, source_target_pairs={{0,1},{1,2},{2,3},{3,0},{4,5},{5,6},{6,7},{7,4},{8,9},{9,10},{10,1... | collective-permute-start | bytes 4616 | tf_op jit(solution)/shard_map/ppermute | solution.py:26
  225.6 5.9 %collective-permute-start.5 = (f32[24,4,4,1]{3,2,1,0:T(4,128)S(1)}, f32[24,4,4,1]{3,2,1,0:T(4,128)S(1)}, u32[]{:S(2)}, u32[]{:S(2)}) collective-permute-start(f32[24,4,4,1]{3,2,1,0:T(4,128)S(1)} %get-tuple-element.706), channel_id=1, source_target_pairs={{1,0},{2,1},{3,2},{0,3},{5,4},{6,5},{7,6},{4,7},{9,8},{10,9},{11,1... | collective-permute-start | bytes 4616 | tf_op jit(solution)/shard_map/ppermute | solution.py:28
  232.1 5.2 copy-start.26
  240.6 2.5 copy-start.32
  257.3 7.0 %collective-permute-start.12 = (f32[24,4,4,1]{3,2,1,0:T(4,128)S(1)}, f32[24,4,4,1]{3,2,1,0:T(4,128)S(1)}, u32[]{:S(2)}, u32[]{:S(2)}) collective-permute-start(f32[24,4,4,1]{3,2,1,0:T(4,128)S(1)} %get-tuple-element.704), channel_id=1, source_target_pairs={{0,3},{1,0},{2,1},{3,2},{4,7},{5,4},{6,5},{7,6},{8,11},{9,8},{10,9... | collective-permute-start | bytes 4616 | tf_op jit(solution)/shard_map/ppermute | solution.py:37
  260.5 12.7 %collective-permute-start.13 = (f32[24,4,4,1]{3,2,1,0:T(4,128)S(1)}, f32[24,4,4,1]{3,2,1,0:T(4,128)S(1)}, u32[]{:S(2)}, u32[]{:S(2)}) collective-permute-start(f32[24,4,4,1]{3,2,1,0:T(4,128)S(1)} %get-tuple-element.703), channel_id=1, source_target_pairs={{0,1},{1,2},{2,3},{3,0},{4,5},{5,6},{6,7},{7,4},{8,9},{9,10},{10,1... | collective-permute-start | bytes 4616 | tf_op jit(solution)/shard_map/ppermute | solution.py:37
  275.9 11.2 %collective-permute-start.14 = (f32[24,4,1,32]{3,2,1,0:T(1,128)S(1)}, f32[24,4,1,32]{3,2,1,0:T(1,128)S(1)}, u32[]{:S(2)}, u32[]{:S(2)}) collective-permute-start(f32[24,4,1,32]{3,2,1,0:T(1,128)S(1)} %get-tuple-element.702), channel_id=1, source_target_pairs={{0,28},{4,0},{8,4},{12,8},{16,12},{20,16},{24,20},{28,24},{1,29},{... | collective-permute-start | bytes 36872 | tf_op jit(solution)/shard_map/ppermute | solution.py:37
  282.4 6.7 %collective-permute-start.15 = (f32[24,4,1,32]{3,2,1,0:T(1,128)S(1)}, f32[24,4,1,32]{3,2,1,0:T(1,128)S(1)}, u32[]{:S(2)}, u32[]{:S(2)}) collective-permute-start(f32[24,4,1,32]{3,2,1,0:T(1,128)S(1)} %get-tuple-element.701), channel_id=1, source_target_pairs={{0,4},{4,8},{8,12},{12,16},{16,20},{20,24},{24,28},{28,0},{1,5},{5... | collective-permute-start | bytes 36872 | tf_op jit(solution)/shard_map/ppermute | solution.py:37
  291.1 2.8 collective-permute-start.16
  292.9 4.9 collective-permute-start.17
  297.8 10.0 %copy-start.12 = (f32[24,2,2,32]{3,2,1,0:T(2,128)}, f32[24,2,2,32]{3,2,1,0:T(2,128)S(1)}, u32[]{:S(2)}) copy-start(f32[24,2,2,32]{3,2,1,0:T(2,128)S(1)} %fusion.203) | copy-start | bytes 36868
  297.8 4.9 collective-permute-start.18
  297.9 4.8 collective-permute-start.19
  302.9 4.9 collective-permute-start.20
  305.4 3.5 collective-permute-start.21
  309.3 7.3 %collective-permute-start.22 = (f32[24,4,4,1]{3,2,1,0:T(4,128)S(1)}, f32[24,4,4,1]{3,2,1,0:T(4,128)S(1)}, u32[]{:S(2)}, u32[]{:S(2)}) collective-permute-start(f32[24,4,4,1]{3,2,1,0:T(4,128)S(1)} %get-tuple-element.699), channel_id=1, source_target_pairs={{0,1},{1,2},{2,3},{3,0},{4,5},{5,6},{6,7},{7,4},{8,9},{9,10},{10,1... | collective-permute-start | bytes 4616 | tf_op jit(solution)/shard_map/ppermute | solution.py:26
  312.9 9.2 %collective-permute-start.23 = (f32[24,4,4,1]{3,2,1,0:T(4,128)S(1)}, f32[24,4,4,1]{3,2,1,0:T(4,128)S(1)}, u32[]{:S(2)}, u32[]{:S(2)}) collective-permute-start(f32[24,4,4,1]{3,2,1,0:T(4,128)S(1)} %get-tuple-element.700), channel_id=1, source_target_pairs={{1,0},{2,1},{3,2},{0,3},{5,4},{6,5},{7,6},{4,7},{9,8},{10,9},{11,1... | collective-permute-start | bytes 4616 | tf_op jit(solution)/shard_map/ppermute | solution.py:28
  322.8 5.2 copy-start.28
  347.9 7.1 %collective-permute-start.24 = (f32[24,4,4,1]{3,2,1,0:T(4,128)S(1)}, f32[24,4,4,1]{3,2,1,0:T(4,128)S(1)}, u32[]{:S(2)}, u32[]{:S(2)}) collective-permute-start(f32[24,4,4,1]{3,2,1,0:T(4,128)S(1)} %get-tuple-element.698), channel_id=1, source_target_pairs={{0,3},{1,0},{2,1},{3,2},{4,7},{5,4},{6,5},{7,6},{8,11},{9,8},{10,9... | collective-permute-start | bytes 4616 | tf_op jit(solution)/shard_map/ppermute | solution.py:37
  348.2 15.8 %collective-permute-start.25 = (f32[24,4,4,1]{3,2,1,0:T(4,128)S(1)}, f32[24,4,4,1]{3,2,1,0:T(4,128)S(1)}, u32[]{:S(2)}, u32[]{:S(2)}) collective-permute-start(f32[24,4,4,1]{3,2,1,0:T(4,128)S(1)} %get-tuple-element.697), channel_id=1, source_target_pairs={{0,1},{1,2},{2,3},{3,0},{4,5},{5,6},{6,7},{7,4},{8,9},{9,10},{10,1... | collective-permute-start | bytes 4616 | tf_op jit(solution)/shard_map/ppermute | solution.py:37
  355.2 31.3 %copy-start.13 = (f32[24,2,2,32]{3,2,1,0:T(2,128)S(1)}, f32[24,2,2,32]{3,2,1,0:T(2,128)}, u32[]{:S(2)}) copy-start(f32[24,2,2,32]{3,2,1,0:T(2,128)} %copy-done.12) | copy-start | bytes 36868
  355.2 31.3 %copy-start.21 = (f32[8,3,2,2,32]{4,3,2,1,0:T(2,128)S(1)}, f32[8,3,2,2,32]{4,3,2,1,0:T(2,128)}, u32[]{:S(2)}) copy-start(f32[8,3,2,2,32]{4,3,2,1,0:T(2,128)} %param.63) | copy-start | bytes 36868
  366.7 9.6 %collective-permute-start.26 = (f32[24,4,1,32]{3,2,1,0:T(1,128)S(1)}, f32[24,4,1,32]{3,2,1,0:T(1,128)S(1)}, u32[]{:S(2)}, u32[]{:S(2)}) collective-permute-start(f32[24,4,1,32]{3,2,1,0:T(1,128)S(1)} %get-tuple-element.696), channel_id=1, source_target_pairs={{0,28},{4,0},{8,4},{12,8},{16,12},{20,16},{24,20},{28,24},{1,29},{... | collective-permute-start | bytes 36872 | tf_op jit(solution)/shard_map/ppermute | solution.py:37
  369.1 9.2 %collective-permute-start.27 = (f32[24,4,1,32]{3,2,1,0:T(1,128)S(1)}, f32[24,4,1,32]{3,2,1,0:T(1,128)S(1)}, u32[]{:S(2)}, u32[]{:S(2)}) collective-permute-start(f32[24,4,1,32]{3,2,1,0:T(1,128)S(1)} %get-tuple-element.695), channel_id=1, source_target_pairs={{0,4},{4,8},{8,12},{12,16},{16,20},{20,24},{24,28},{28,0},{1,5},{5... | collective-permute-start | bytes 36872 | tf_op jit(solution)/shard_map/ppermute | solution.py:37
  380.3 2.8 collective-permute-start.28
  381.7 4.9 collective-permute-start.29
  387.3 4.9 collective-permute-start.30
  387.4 4.8 collective-permute-start.31
  392.3 7.3 %collective-permute-start.32 = (f32[24,4,1,32]{3,2,1,0:T(1,128)S(1)}, f32[24,4,1,32]{3,2,1,0:T(1,128)S(1)}, u32[]{:S(2)}, u32[]{:S(2)}) collective-permute-start(f32[24,4,1,32]{3,2,1,0:T(1,128)S(1)} %get-tuple-element.709), channel_id=1, source_target_pairs={{0,4},{4,8},{8,12},{12,16},{16,20},{20,24},{24,28},{28,0},{1,5},{5... | collective-permute-start | bytes 36872 | tf_op jit(solution)/shard_map/ppermute | solution.py:26
  395.0 4.8 collective-permute-start.33
  400.2 7.6 %collective-permute-start.34 = (f32[24,4,4,1]{3,2,1,0:T(4,128)S(1)}, f32[24,4,4,1]{3,2,1,0:T(4,128)S(1)}, u32[]{:S(2)}, u32[]{:S(2)}) collective-permute-start(f32[24,4,4,1]{3,2,1,0:T(4,128)S(1)} %get-tuple-element.693), channel_id=1, source_target_pairs={{0,1},{1,2},{2,3},{3,0},{4,5},{5,6},{6,7},{7,4},{8,9},{9,10},{10,1... | collective-permute-start | bytes 4616 | tf_op jit(solution)/shard_map/ppermute | solution.py:26
  400.3 8.2 %collective-permute-start.35 = (f32[24,4,4,1]{3,2,1,0:T(4,128)S(1)}, f32[24,4,4,1]{3,2,1,0:T(4,128)S(1)}, u32[]{:S(2)}, u32[]{:S(2)}) collective-permute-start(f32[24,4,4,1]{3,2,1,0:T(4,128)S(1)} %get-tuple-element.694), channel_id=1, source_target_pairs={{1,0},{2,1},{3,2},{0,3},{5,4},{6,5},{7,6},{4,7},{9,8},{10,9},{11,1... | collective-permute-start | bytes 4616 | tf_op jit(solution)/shard_map/ppermute | solution.py:28
  409.1 5.2 copy-start.24
  417.6 2.5 copy-start.34
  417.6 2.5 copy-start.37
  424.7 4.1 copy-start.18
  424.7 4.1 copy-start.19
  432.6 9.9 %collective-permute-start.36 = (f32[24,4,4,1]{3,2,1,0:T(4,128)S(1)}, f32[24,4,4,1]{3,2,1,0:T(4,128)S(1)}, u32[]{:S(2)}, u32[]{:S(2)}) collective-permute-start(f32[24,4,4,1]{3,2,1,0:T(4,128)S(1)} %get-tuple-element.692), channel_id=1, source_target_pairs={{0,3},{1,0},{2,1},{3,2},{4,7},{5,4},{6,5},{7,6},{8,11},{9,8},{10,9... | collective-permute-start | bytes 4616 | tf_op jit(solution)/shard_map/ppermute | solution.py:37
  437.9 13.5 %collective-permute-start.37 = (f32[24,4,4,1]{3,2,1,0:T(4,128)S(1)}, f32[24,4,4,1]{3,2,1,0:T(4,128)S(1)}, u32[]{:S(2)}, u32[]{:S(2)}) collective-permute-start(f32[24,4,4,1]{3,2,1,0:T(4,128)S(1)} %get-tuple-element.691), channel_id=1, source_target_pairs={{0,1},{1,2},{2,3},{3,0},{4,5},{5,6},{6,7},{7,4},{8,9},{9,10},{10,1... | collective-permute-start | bytes 4616 | tf_op jit(solution)/shard_map/ppermute | solution.py:37
  442.6 36.1 %copy-start.14 = (f32[24,2,2,32]{3,2,1,0:T(2,128)S(1)}, f32[24,2,2,32]{3,2,1,0:T(2,128)}, u32[]{:S(2)}) copy-start(f32[24,2,2,32]{3,2,1,0:T(2,128)} %copy-done.12) | copy-start | bytes 36868
  451.4 27.4 %copy-start.23 = (f32[8,3,2,2,32]{4,3,2,1,0:T(2,128)S(1)}, f32[8,3,2,2,32]{4,3,2,1,0:T(2,128)}, u32[]{:S(2)}) copy-start(f32[8,3,2,2,32]{4,3,2,1,0:T(2,128)} %get-tuple-element.595) | copy-start | bytes 36868
  451.4 28.1 %copy-start.22 = (f32[8,3,2,2,32]{4,3,2,1,0:T(2,128)S(1)}, f32[8,3,2,2,32]{4,3,2,1,0:T(2,128)}, u32[]{:S(2)}) copy-start(f32[8,3,2,2,32]{4,3,2,1,0:T(2,128)} %param.63) | copy-start | bytes 36868
  451.4 28.1 %copy-start.30 = (f32[8,3,2,2,32]{4,3,2,1,0:T(2,128)S(1)}, f32[8,3,2,2,32]{4,3,2,1,0:T(2,128)}, u32[]{:S(2)}) copy-start(f32[8,3,2,2,32]{4,3,2,1,0:T(2,128)} %get-tuple-element.768) | copy-start | bytes 36868
  454.1 9.8 %collective-permute-start.38 = (f32[24,4,1,32]{3,2,1,0:T(1,128)S(1)}, f32[24,4,1,32]{3,2,1,0:T(1,128)S(1)}, u32[]{:S(2)}, u32[]{:S(2)}) collective-permute-start(f32[24,4,1,32]{3,2,1,0:T(1,128)S(1)} %get-tuple-element.690), channel_id=1, source_target_pairs={{0,28},{4,0},{8,4},{12,8},{16,12},{20,16},{24,20},{28,24},{1,29},{... | collective-permute-start | bytes 36872 | tf_op jit(solution)/shard_map/ppermute | solution.py:37
  460.6 5.9 %collective-permute-start.39 = (f32[24,4,1,32]{3,2,1,0:T(1,128)S(1)}, f32[24,4,1,32]{3,2,1,0:T(1,128)S(1)}, u32[]{:S(2)}, u32[]{:S(2)}) collective-permute-start(f32[24,4,1,32]{3,2,1,0:T(1,128)S(1)} %get-tuple-element.689), channel_id=1, source_target_pairs={{0,4},{4,8},{8,12},{12,16},{16,20},{20,24},{24,28},{28,0},{1,5},{5... | collective-permute-start | bytes 36872 | tf_op jit(solution)/shard_map/ppermute | solution.py:37
  468.5 6.3 %collective-permute-start.40 = (f32[24,1,2,32]{3,2,1,0:T(2,128)S(1)}, f32[24,1,2,32]{3,2,1,0:T(2,128)S(1)}, u32[]{:S(2)}, u32[]{:S(2)}) collective-permute-start(f32[24,1,2,32]{3,2,1,0:T(2,128)S(1)} %get-tuple-element.708), channel_id=1, source_target_pairs={{0,224},{32,0},{64,32},{96,64},{128,96},{160,128},{192,160},{224,1... | collective-permute-start | bytes 18440 | tf_op jit(solution)/shard_map/ppermute | solution.py:37
  473.8 4.9 collective-permute-start.41
  (29 other events, 57.0 us)
where the time goes:
time: 563 us; the launch traced here: 557 us
  local copies, waits for them, and re-layouts  184 us (33%)
  matrix products  101 us (18%)
  starting transfers between devices  96.4 us (17%)
  blocking collectives  76.1 us (14%)
  waiting for transfers between devices  60 us (11%)
  other arithmetic  32.5 us (6%)
    dynamic_update_slice x52, local copies, waits for them, and re-layouts, on_device(): lax.scan(code_tables, jnp.zeros((centre_count, channels), jnp.float32), (...  115 us
    psum x1, blocking collectives, record(): return lax.psum(local_term, ('gx', 'gy', 'gz'))  76.1 us
    ppermute x18, starting transfers between devices, from_behind(): lax.ppermute(value, axis, [(i, (i + by) % size) for i in range(size)])  46.3 us
    scatter-add x12, local copies, waits for them, and re-layouts, fold_dim(): interior = interior.at[tuple(selector)].add(arrived)  45.2 us
    ppermute x18, waiting for transfers between devices, from_behind(): lax.ppermute(value, axis, [(i, (i + by) % size) for i in range(size)])  30.5 us
    ppermute x12, starting transfers between devices, padded_2(): lax.ppermute(head, axis, [((i + 1) % count, i) for i in range(count)])  27.8 us
    dot_general x78, matrix products, radial(): return jnp.dot(hidden, w_radial2, precision=HIGHEST) * envelope[..., None]  24.1 us
    ppermute x12, starting transfers between devices, padded_2(): lax.ppermute(tail, axis, [(i, (i + 1) % count) for i in range(count)])  22.3 us
  transfers between devices with their start and end apart: 42, of which 30 were waited for; matrix products, arithmetic and copies ran while one was open for 40% of the time, Pallas kernels for 0%

commit v1 on v0

v1 whole, which is shorter than its diff:
```python
import functools
import math

import jax
import jax.numpy as jnp
from jax import lax
from jax.experimental import pallas as pl
from jax.experimental.pallas import tpu as pltpu
from jax.sharding import PartitionSpec as P

SPACING = 2.2
CUTOFF = 5.0
NORM_SCALE = 0.22360679774997896
MASSES = (28.0855, 15.999, 22.99)
HIGHEST = lax.Precision.HIGHEST
MESH = pl.DeviceIdType.MESH
F32 = jnp.float32
BF16 = jnp.bfloat16

CODES = tuple(c for c in range(27) if c != 13)
ORDER = {c: n for n, c in enumerate(CODES)}
NC = len(CODES)
AXES = ("gx", "gy", "gz")
LANES = 128
HID = 64
PROBES = 8


def step_of(code):
    return code // 9 - 1, code // 3 % 3 - 1, code % 3 - 1


def roll(value, by):
    return pltpu.roll(value, by % LANES, 1)


def high_low(value):
    high = value.astype(BF16).astype(F32)
    return high, value - high


def by_species(species, values):
    return jnp.where(species < 0.5, values[0], jnp.where(species < 1.5, values[1], values[2]))


def sin_cos(angle):
    off = angle - math.pi / 2
    square = off * off
    odd = jnp.full_like(off, -1.0 / math.factorial(15))
    for power in (13, 11, 9, 7, 5, 3, 1):
        odd = odd * square + (-1.0) ** (power // 2) / math.factorial(power)
    even = jnp.full_like(off, 1.0 / math.factorial(16))
    for power in (14, 12, 10, 8, 6, 4, 2, 0):
        even = even * square + (-1.0) ** (power // 2) / math.factorial(power)
    return even, -odd * off


class Lanes:
    def __init__(self):
        lane = lax.broadcasted_iota(jnp.int32, (8, LANES), 1)
        self.lane = lane
        self.x = lane >= 64
        self.y = (lane & 32) != 0
        self.z = lane & 31
        self.z_low = self.z == 0
        self.z_high = self.z == 31

    def swap(self, axis, value):
        if axis == 0:
            return roll(value, 64)
        return jnp.where(self.y, roll(value, 32), roll(value, -32))

    def upper(self, axis):
        return self.x if axis == 0 else self.y


def gather(lanes, ext):
    along_x = {}
    for gy in (0, 1):
        for gz in (0, 1):
            own, ghost = ext[0][gy][gz], ext[1][gy][gz]
            along_x[0, gy, gz] = own
            along_x[1, gy, gz] = lanes.swap(0, jnp.where(lanes.x, own, ghost))
            along_x[-1, gy, gz] = lanes.swap(0, jnp.where(lanes.x, ghost, own))
    out = {}
    for sx in (-1, 0, 1):
        along_y = {}
        for gz in (0, 1):
            own, ghost = along_x[sx, 0, gz], along_x[sx, 1, gz]
            along_y[0, gz] = own
            along_y[1, gz] = lanes.swap(1, jnp.where(lanes.y, own, ghost))
            along_y[-1, gz] = lanes.swap(1, jnp.where(lanes.y, ghost, own))
        for sy in (-1, 0, 1):
            own, ghost = along_y[sy, 0], along_y[sy, 1]
            base = (sx + 1) * 9 + (sy + 1) * 3 + 1
            out[base] = own
            out[base + 1] = jnp.where(lanes.z_high, roll(ghost, 31), roll(own, -1))
            out[base - 1] = jnp.where(lanes.z_low, roll(ghost, -31), roll(own, 1))
    return out


def scatter(lanes, edges):
    along_z = {}
    for sx in (-1, 0, 1):
        for sy in (-1, 0, 1):
            base = (sx + 1) * 9 + (sy + 1) * 3 + 1
            up, down = edges(base + 1), edges(base - 1)
            own = edges(base)
            own = own + jnp.where(lanes.z_low, 0.0, roll(up, 1))
            own = own + jnp.where(lanes.z_high, 0.0, roll(down, -1))
            ghost = jnp.where(
                lanes.z_low, roll(up, -31), jnp.where(lanes.z_high, roll(down, 31), 0.0)
            )
            along_z[sx, sy, 0], along_z[sx, sy, 1] = own, ghost
    along_y = {}
    for sx in (-1, 0, 1):
        for gz in (0, 1):
            up, down = along_z[sx, 1, gz], along_z[sx, -1, gz]
            along_y[sx, 0, gz] = along_z[sx, 0, gz] + lanes.swap(1, jnp.where(lanes.y, down, up))
            along_y[sx, 1, gz] = lanes.swap(1, jnp.where(lanes.y, up, down))
    ext = [[[None, None], [None, None]], [[None, None], [None, None]]]
    for gy in (0, 1):
        for gz in (0, 1):
            up, down = along_y[1, gy, gz], along_y[-1, gy, gz]
            ext[0][gy][gz] = along_y[0, gy, gz] + lanes.swap(0, jnp.where(lanes.x, down, up))
            ext[1][gy][gz] = lanes.swap(0, jnp.where(lanes.x, up, down))
    return ext


def kernel(
    sizes,
    radius_ref,
    pack_ref,
    emb_ref,
    w1_ref,
    w2_ref,
    wn_ref,
    readout_ref,
    cheb_ref,
    moments_ref,
    halo_send,
    halo_recv,
    fold_send,
    fold_recv,
    sum_send,
    sum_recv,
    halo_sems,
    fold_sems,
    sum_sems,
    geo_ref,
    trig_ref,
    rows_ref,
    acc_ref,
    prod_ref,
    second_ref,
    node_ref,
    matrix_ref,
    dv_ref,
    dr_ref,
    edge_ref,
    small_ref,
):
    place = [lax.axis_index(axis) for axis in AXES]

    def partner(axis, by):
        return lax.rem(place[axis] + (by + sizes[axis]), sizes[axis])

    barrier = pltpu.get_barrier_semaphore()
    partners = [(axis, by) for axis in range(3) for by in range(1, sizes[axis])]
    for axis, by in partners:
        pl.semaphore_signal(
            barrier, inc=1, device_id={AXES[axis]: partner(axis, by)}, device_id_type=MESH
        )

    lanes = Lanes()
    species = pack_ref[3:4, :]
    inv_root = by_species(species, [1.0 / math.sqrt(m) for m in MASSES])
    root = by_species(species, [math.sqrt(m) for m in MASSES])
    probes = [pack_ref[pl.ds(8 + j, PROBES, stride=3), :] for j in range(3)]
    start = [p * inv_root for p in probes]
    own_halo = start + [pack_ref[0:8, :]]

    pl.semaphore_wait(barrier, len(partners))

    def copy(src, dst, sems, number, axis, by):
        return pltpu.make_async_remote_copy(
            src_ref=src,
            dst_ref=dst,
            send_sem=sems.at[0, number],
            recv_sem=sems.at[1, number],
            device_id={AXES[axis]: partner(axis, by)},
            device_id_type=MESH,
        )

    def merge(axis, low_value, high_value):
        if axis < 2:
            return jnp.where(lanes.upper(axis), high_value, low_value)
        return jnp.where(lanes.z_low, low_value, jnp.where(lanes.z_high, high_value, 0.0))

    def halo_start(axis, held):
        for n, array in enumerate(held):
            for v in range(4):
                halo_send[axis, pl.ds(8 * (4 * n + v), 8), :] = array[v]
        rows = pl.ds(0, 32 * len(held))
        copies = [
            copy(
                halo_send.at[axis, rows],
                halo_recv.at[axis, d, rows],
                halo_sems,
                2 * axis + d,
                axis,
                1 if d == 0 else -1,
            )
            for d in (0, 1)
        ]
        for c in copies:
            c.start()
        return copies

    def halo_finish(axis, held, copies):
        for c in copies:
            c.wait()
        ghosts = []
        for n in range(len(held)):
            ghost = []
            for v in range(4):
                rows = pl.ds(8 * (4 * n + v), 8)
                ghost.append(merge(axis, halo_recv[axis, 1, rows, :], halo_recv[axis, 0, rows, :]))
            ghosts.append(ghost)
        return held + ghosts

    held = [own_halo]
    copies = halo_start(0, held)

    for s in range(3):
        acc_ref[pl.ds(64 * s, 64), :] = w2_ref[...] * emb_ref[s : s + 1, :]
    to_node = jnp.dot(
        acc_ref[...], wn_ref[...], precision=HIGHEST, preferred_element_type=F32
    ) * NORM_SCALE
    flipped = [jnp.transpose(to_node[64 * s : 64 * s + 64, :]) for s in range(3)]
    flip = [high_low(f) for f in flipped]
    left_node = jnp.concatenate(
        [jnp.concatenate([hi, hi, lo], axis=1) for hi, lo in flip], axis=0
    ).astype(BF16)
    first_high, first_low = high_low(w1_ref[...] * math.sqrt(2.0 / CUTOFF))
    left_radial = jnp.transpose(
        jnp.concatenate([first_high, first_high, first_low, jnp.zeros_like(first_high)], axis=0)
    ).astype(BF16)
    small_ref[0:8, :] = jnp.zeros((8, LANES), F32)
    small_ref[0:3, :] = emb_ref[...]
    small_ref[3:4, :] = readout_ref[...]
    columns = jnp.transpose(small_ref[0:8, :])
    readout = columns[:, 3:4]

    row_lane = lax.broadcasted_iota(jnp.int32, (32, LANES), 1)
    home = (
        ((row_lane >> 6) + 1) * (4 * 34) + (((row_lane >> 5) & 1) + 1) * 34 + (row_lane & 31) + 1
    )
    off = pack_ref[32:64, :].astype(jnp.int32) - home

    def unit(value, bound):
        return jnp.where(value > bound, 1, 0) - jnp.where(value < -bound, 1, 0)

    off_x = unit(off, 68)
    rest = off - 136 * off_x
    off_y = unit(rest, 17)
    off_z = rest - 34 * off_y
    code = (off_x + 1) * 9 + (off_y + 1) * 3 + off_z + 1
    bits = jnp.where(off == 0, 0, jnp.left_shift(jnp.ones_like(code), code))
    bits = jnp.sum(bits, axis=0, keepdims=True)

    for axis in range(3):
        held = halo_finish(axis, held, copies)
        if axis < 2:
            copies = halo_start(axis + 1, held)

    def ext_of(v):
        return [[[held[gx + 2 * gy + 4 * gz][v] for gz in (0, 1)] for gy in (0, 1)] for gx in (0, 1)]

    geometry = ext_of(3)
    y_old = [ext_of(j) for j in range(3)]
    scale = 1.0 / radius_ref[0]
    weight_sq = [
        [
            [by_species(geometry[gx][gy][gz][3:4, :], [1.0 / m for m in MASSES]) * scale for gz in (0, 1)]
            for gy in (0, 1)
        ]
        for gx in (0, 1)
    ]

    seen = gather(lanes, geometry)
    for n, c in enumerate(CODES):
        geo_ref[pl.ds(8 * n, 8), :] = seen[c]
        rows_ref[9, pl.ds(n, 1), :] = (jnp.right_shift(bits, c) & 1).astype(F32)
    code_row = lax.broadcasted_iota(jnp.int32, (NC, LANES), 0)
    code_row = code_row + jnp.where(code_row >= 13, 1, 0)
    off_z = code_row % 3
    off_y = (code_row // 3) % 3
    off_x = code_row // 9
    vectors = []
    for j, steps in enumerate((off_x, off_y, off_z)):
        vectors.append(
            (steps - 1).astype(F32) * SPACING
            + geo_ref[pl.ds(j, NC, stride=8), :]
            - pack_ref[j : j + 1, :]
        )
    filled = rows_ref[9, 0:NC, :]
    present = filled > 0.5
    square = vectors[0] * vectors[0] + vectors[1] * vectors[1] + vectors[2] * vectors[2]
    distance = jnp.sqrt(jnp.where(present, square, 1.0))
    inverse = 1.0 / distance
    part = distance * (1.0 / CUTOFF)
    part_sq = part * part
    for j in range(3):
        rows_ref[j, 0:NC, :] = vectors[j] * inverse
    rows_ref[3, 0:NC, :] = inverse
    rows_ref[4, 0:NC, :] = filled * (1.0 - part_sq) * (1.0 - part_sq)
    rows_ref[5, 0:NC, :] = filled * (-4.0 / CUTOFF) * part * (1.0 - part_sq)
    rows_ref[6, 0:NC, :] = filled * (-4.0 / CUTOFF**2) * (1.0 - 3.0 * part_sq)
    rows_ref[7, 0:NC, :] = geo_ref[pl.ds(3, NC, stride=8), :]
    sin_1, cos_1 = sin_cos(distance * (math.pi / CUTOFF))
    sin_k, cos_k = sin_1, cos_1
    sin_b, cos_b = jnp.zeros_like(sin_1), jnp.ones_like(cos_1)
    for k in range(8):
        omega = (k + 1) * math.pi / CUTOFF
        trig_ref[pl.ds(k, NC, stride=24), :] = sin_k
        trig_ref[pl.ds(8 + k, NC, stride=24), :] = cos_k * omega
        trig_ref[pl.ds(16 + k, NC, stride=24), :] = sin_k * (-omega * omega)
        sin_k, sin_b = 2.0 * cos_1 * sin_k - sin_b, sin_k
        cos_k, cos_b = 2.0 * cos_1 * cos_k - cos_b, cos_k

    acc_ref[...] = jnp.zeros_like(acc_ref)

    def radial(pair, carry):
        blocks = []
        for i in (0, 1):
            for g in range(3):
                hi, lo = high_low(trig_ref[pl.ds((2 * pair + i) * 24 + 8 * g, 8), :])
                blocks.append(jnp.concatenate([hi, lo, hi, jnp.zeros_like(hi)], axis=0))
        right = jnp.concatenate(blocks, axis=1).astype(BF16)
        waves = jnp.dot(left_radial, right, preferred_element_type=F32)
        rights = []
        for i in (0, 1):
            n = 2 * pair + i
            wave = [waves[:, 128 * (3 * i + g) : 128 * (3 * i + g + 1)] for g in range(3)]
            inv = rows_ref[3, pl.ds(n, 1), :]
            env = [rows_ref[4 + g, pl.ds(n, 1), :] for g in range(3)]
            kind = rows_ref[7, pl.ds(n, 1), :]
            x_0 = wave[0] * inv
            x_1 = (wave[1] - x_0) * inv
            x_2 = (wave[2] - 2.0 * x_1) * inv
            gate = 1.0 / (1.0 + jnp.exp(-x_0))
            shut = 1.0 - gate
            value = x_0 * gate
            slope = gate + value * shut
            bend = shut * (2.0 * gate + value * (1.0 - 2.0 * gate))
            r_1 = slope * x_1
            r_2 = bend * x_1 * x_1 + slope * x_2
            h_0 = value * env[0]
            h_1 = r_1 * env[0] + value * env[1]
            h_2 = r_2 * env[0] + 2.0 * r_1 * env[1] + value * env[2]
            second_ref[n] = h_2
            for s in range(3):
                one = jnp.where(jnp.abs(kind - s) < 0.5, 1.0, 0.0)
                acc_ref[pl.ds(64 * s, 64), :] += h_0 * one
            hi, lo = high_low(h_1)
            rights.append(jnp.concatenate([hi, lo, hi], axis=0).astype(BF16))
        product = jnp.dot(
            left_node, jnp.concatenate(rights, axis=1), preferred_element_type=F32
        )
        for i in (0, 1):
            n = 2 * pair + i
            kind = rows_ref[7, pl.ds(n, 1), :]
            cols = slice(128 * i, 128 * i + 128)
            prod_ref[n] = by_species(
                kind, [product[128 * s : 128 * s + 128, cols] for s in range(3)]
            )
        return carry

    lax.fori_loop(0, NC // 2, radial, 0)

    home_kind = jnp.where(
        lax.broadcasted_iota(jnp.int32, (8, LANES), 0).astype(F32) == species, 1.0, 0.0
    )
    home_kind = jnp.where(lax.broadcasted_iota(jnp.int32, (8, LANES), 0) < 3, home_kind, 0.0)
    node = jnp.dot(columns, home_kind, precision=HIGHEST, preferred_element_type=F32)
    node = node + jnp.dot(
        jnp.concatenate(flipped, axis=1), acc_ref[...], precision=HIGHEST, preferred_element_type=F32
    )
    gate = 1.0 / (1.0 + jnp.exp(-node))
    shut = 1.0 - gate
    value = node * gate
    node_slope = readout * (gate + value * shut)
    node_ref[0] = node_slope
    node_ref[1] = readout * (shut * (2.0 * gate + value * (1.0 - 2.0 * gate)))
    acc_ref[...] = jnp.dot(to_node, node_slope, precision=HIGHEST, preferred_element_type=F32)

    def edge_matrix(n, carry):
        mine = prod_ref[n]
        kind = rows_ref[7, pl.ds(n, 1), :]
        pull = jnp.sum(mine * node_ref[0], axis=0, keepdims=True) * rows_ref[3, pl.ds(n, 1), :]
        back = by_species(kind, [acc_ref[64 * s : 64 * s + 64, :] for s in range(3)])
        curve = jnp.sum(back * second_ref[n], axis=0, keepdims=True)
        rows_ref[8, pl.ds(n, 1), :] = pull
        bent = mine * node_ref[1]
        for m in range(NC):
            both = jnp.sum(bent * prod_ref[m], axis=0, keepdims=True)
            matrix_ref[n * NC + m] = jnp.broadcast_to(both, (8, LANES))
        matrix_ref[n * NC + n] = matrix_ref[n * NC + n] + (curve - pull)
        return carry

    lax.fori_loop(0, NC, edge_matrix, 0)

    def local_product(y):
        for j in range(3):
            views = gather(lanes, y[j])
            for n, c in enumerate(CODES):
                dv_ref[3 * n + j] = views[c] - views[13]

        def along(n, carry):
            total = jnp.zeros((8, LANES), F32)
            for j in range(3):
                total = total + rows_ref[j, pl.ds(n, 1), :] * dv_ref[3 * n + j]
            dr_ref[n] = total
            return carry

        lax.fori_loop(0, NC, along, 0, unroll=True)

        def force(n, carry):
            total = matrix_ref[n * NC] * dr_ref[0]
            for m in range(1, NC):
                total = total + matrix_ref[n * NC + m] * dr_ref[m]
            pull = rows_ref[8, pl.ds(n, 1), :]
            out = []
            for j in range(3):
                edge = rows_ref[j, pl.ds(n, 1), :] * total + pull * dv_ref[3 * n + j]
                edge_ref[3 * n + j] = edge
                out.append(carry[j] - edge)
            return tuple(out)

        zero = jnp.zeros((8, LANES), F32)
        centre = lax.fori_loop(0, NC, force, (zero, zero, zero))
        return [
            scatter(lanes, lambda c, j=j: centre[j] if c == 13 else edge_ref[3 * ORDER[c] + j])
            for j in range(3)
        ]

    def exchange(number, terms, own_only, beside):
        held = {
            (gx, gy, gz): [terms[j][gx][gy][gz] for j in range(3)]
            for gx in (0, 1)
            for gy in (0, 1)
            for gz in (0, 1)
        }
        for axis in range(3):
            owns = sorted(k for k in held if k[axis] == 0)
            count = 3 * len(owns)
            for n, key in enumerate(owns):
                other = key[:axis] + (1,) + key[axis + 1 :]
                for j in range(3):
                    own, ghost = held[key][j], held[other][j]
                    rows = pl.ds(8 * (3 * n + j), 8)
                    if axis < 2:
                        low = jnp.logical_not(lanes.upper(axis))
                        high = lanes.upper(axis)
                    else:
                        low, high = lanes.z_low, lanes.z_high
                    fold_send[number, axis, 0, rows, :] = jnp.where(low, ghost, own)
                    fold_send[number, axis, 1, rows, :] = jnp.where(high, ghost, own)
            rows = pl.ds(0, 8 * count)
            copies = [
                copy(
                    fold_send.at[number, axis, d, rows],
                    fold_recv.at[number, axis, d, rows],
                    fold_sems.at[number],
                    2 * axis + d,
                    axis,
                    1 if d == 0 else -1,
                )
                for d in (0, 1)
            ]
            for c in copies:
                c.start()
            beside(axis)
            for c in copies:
                c.wait()
            after = {}
            for n, key in enumerate(owns):
                other = key[:axis] + (1,) + key[axis + 1 :]
                own_sum, ghost_sum = [], []
                for j in range(3):
                    rows = pl.ds(8 * (3 * n + j), 8)
                    below = fold_recv[number, axis, 0, rows, :]
                    above = fold_recv[number, axis, 1, rows, :]
                    own_sum.append(held[key][j] + merge(axis, below, above))
                    ghost_sum.append(held[other][j] + merge(axis, above, below))
                after[key] = own_sum
                if not own_only:
                    after[other] = ghost_sum
            held = after
        return held

    def advance(product, factor, before):
        return [
            [
                [
                    [
                        product[gx, gy, gz][j] * (weight_sq[gx][gy][gz] * factor)
                        - (0.0 if before is None else before[j][gx][gy][gz])
                        for gz in (0, 1)
                    ]
                    for gy in (0, 1)
                ]
                for gx in (0, 1)
            ]
            for j in range(3)
        ]

    def nothing(axis):
        return None

    product = exchange(0, local_product(y_old), False, nothing)
    y_1 = advance(product, 1.0, None)
    product = exchange(1, local_product(y_1), False, nothing)
    y_2 = advance(product, 2.0, y_old)
    t_1 = [y_1[j][0][0][0] * root for j in range(3)]
    t_2 = [y_2[j][0][0][0] * root for j in range(3)]
    for j in range(3):
        cheb_ref[0, pl.ds(j, PROBES, stride=3), :] = t_2[j]

    terms = [
        sum(probes[j] * probes[j] for j in range(3)),
        sum(probes[j] * t_1[j] for j in range(3)),
        sum(probes[j] * t_2[j] for j in range(3)),
        sum((2.0 * t_2[j] - probes[j]) * t_1[j] for j in range(3)),
    ]
    packed = jnp.zeros((8, LANES), F32)
    for k in range(4):
        packed = jnp.where(lanes.lane == k, jnp.sum(terms[k], axis=1, keepdims=True), packed)
    moments_ref[...] = packed

    def sum_start(axis):
        sum_send[axis] = moments_ref[...]
        copies = []
        for by in range(1, sizes[axis]):
            c = copy(
                sum_send.at[axis],
                sum_recv.at[axis, by],
                sum_sems.at[axis],
                by,
                axis,
                by,
            )
            c.start()
            copies.append(c)
        return copies

    def sum_finish(axis, copies):
        for c in copies:
            c.wait()
        sum_recv[axis, 0] = sum_send[axis]
        total = jnp.zeros((8, LANES), F32)
        for index in range(sizes[axis]):
            slot = lax.rem(place[axis] + (sizes[axis] - index), sizes[axis])
            total = total + sum_recv[axis, slot]
        moments_ref[...] = total

    terms_3 = local_product(y_2)
    flight = {}

    def beside(axis):
        if axis > 0:
            sum_finish(axis - 1, flight.pop(axis - 1))
        flight[axis] = sum_start(axis)

    product = exchange(2, terms_3, True, beside)
    own_weight = weight_sq[0][0][0] * 2.0 * root
    for j in range(3):
        cheb_ref[1, pl.ds(j, PROBES, stride=3), :] = product[0, 0, 0][j] * own_weight - t_1[j]
    sum_finish(2, flight.pop(2))


def on_device(
    sizes,
    displacements,
    species,
    neighbor_index,
    probes,
    embedding,
    w_radial1,
    w_radial2,
    w_node,
    readout,
    spectral_radius,
):
    site = species.shape
    pack = jnp.concatenate(
        [
            displacements,
            species.astype(F32)[None],
            jnp.zeros((4,) + site, F32),
            probes.reshape((3 * PROBES,) + site),
            neighbor_index.astype(F32),
        ],
        axis=0,
    ).reshape(64, LANES)
    vmem = pl.BlockSpec(memory_space=pltpu.VMEM)
    most = max(sizes)
    cheb, moments = pl.pallas_call(
        functools.partial(kernel, sizes),
        out_shape=(
            jax.ShapeDtypeStruct((2, 3 * PROBES, LANES), F32),
            jax.ShapeDtypeStruct((8, LANES), F32),
        ),
        in_specs=[pl.BlockSpec(memory_space=pltpu.SMEM)] + [vmem] * 6,
        out_specs=(vmem, vmem),
        scratch_shapes=[
            pltpu.VMEM((3, 128, LANES), F32),
            pltpu.VMEM((3, 2, 128, LANES), F32),
            pltpu.VMEM((3, 3, 2, 96, LANES), F32),
            pltpu.VMEM((3, 3, 2, 96, LANES), F32),
            pltpu.VMEM((3, 8, LANES), F32),
            pltpu.VMEM((3, most, 8, LANES), F32),
            pltpu.SemaphoreType.DMA((2, 6)),
            pltpu.SemaphoreType.DMA((3, 2, 6)),
            pltpu.SemaphoreType.DMA((3, 2, most)),
            pltpu.VMEM((8 * NC, LANES), F32),
            pltpu.VMEM((24 * NC, LANES), F32),
            pltpu.VMEM((10, 32, LANES), F32),
            pltpu.VMEM((3 * HID, LANES), F32),
            pltpu.VMEM((NC, 128, LANES), F32),
            pltpu.VMEM((NC, HID, LANES), F32),
            pltpu.VMEM((2, 128, LANES), F32),
            pltpu.VMEM((NC * NC, 8, LANES), F32),
            pltpu.VMEM((3 * NC, 8, LANES), F32),
            pltpu.VMEM((NC, 8, LANES), F32),
            pltpu.VMEM((3 * NC, 8, LANES), F32),
            pltpu.VMEM((8, LANES), F32),
        ],
        compiler_params=pltpu.CompilerParams(
            collective_id=0, has_side_effects=True, vmem_limit_bytes=40 * 2**20
        ),
        name="chebyshev",
    )(
        spectral_radius,
        pack,
        embedding,
        w_radial1,
        w_radial2,
        w_node,
        readout.reshape(1, -1),
    )
    return cheb.reshape((2,) + probes.shape), moments[:, :4].T


def solution(mesh):
    placed = (
        P(None, "gx", "gy", "gz"),
        P("gx", "gy", "gz"),
        P(None, "gx", "gy", "gz"),
        P(None, None, "gx", "gy", "gz"),
        P(),
        P(),
        P(),
        P(),
        P(),
        P(),
    )
    return jax.shard_map(
        functools.partial(on_device, tuple(mesh.shape[axis] for axis in AXES)),
        mesh=mesh,
        in_specs=placed,
        out_specs=(P(None, None, None, "gx", "gy", "gz"), P()),
        check_vma=False,
    )
```

time: 563 us -> 78.8 us (0.14); the launches traced: 557 us -> 78.6 us
  local copies, waits for them, and re-layouts: 184 us -> 4.06 us
  matrix products: 101 us -> 0 us
  starting transfers between devices: 96.4 us -> 0 us
  blocking collectives: 76.1 us -> 0 us
  Pallas kernels: 0 us -> 72.4 us
  waiting for transfers between devices: 60 us -> 0 us
  other arithmetic: 32.5 us -> 0.71 us
    dynamic_update_slice x52 -> x0, local copies, waits for them, and re-layouts: 115 us -> none  [on_device(): lax.scan(code_tables, jnp.zeros((centre_count, channels), jnp.float32), (...]
    dot_general x208 -> x0, matrix products: 101 us -> none  [the longest x78 24.1 us: radial(): return jnp.dot(hidden, w_radial2, precision=HIGHEST) * envelope[..., None]]
    ppermute x42 -> x0, starting transfers between devices: 96.4 us -> none  [the longest x18 46.3 us: from_behind(): lax.ppermute(value, axis, [(i, (i + by) % size) for i in range(size)])]
    psum x1 -> x0, blocking collectives: 76.1 us -> none  [record(): return lax.psum(local_term, ('gx', 'gy', 'gz'))]
    pallas_call x0 -> x1, Pallas kernels: none -> 72.4 us  [on_device(): pl.pallas_call(functools.partial(kernel, sizes), out_shape=(jax.ShapeDtyp...]
    ppermute x42 -> x0, waiting for transfers between devices: 60 us -> none  [the longest x18 30.5 us: from_behind(): lax.ppermute(value, axis, [(i, (i + by) % size) for i in range(size)])]
    scatter-add x12 -> x0, local copies, waits for them, and re-layouts: 45.2 us -> none  [fold_dim(): interior = interior.at[tuple(selector)].add(arrived)]
    unnamed x196 -> x13, local copies, waits for them, and re-layouts: 11.8 us -> 1.38 us
  transfers between devices with their start and end apart: 42 -> 0, of which waited for: 30 -> 0; matrix products, arithmetic and copies ran while one was open for 40% -> 0% of each run, Pallas kernels for 0% -> 0%
where the time goes in v1:
time: 78.8 us; the launch traced here: 78.6 us
  Pallas kernels  72.4 us (92%)
  local copies, waits for them, and re-layouts  4.06 us (5%)
  between operations  1.38 us (2%)
    pallas_call x1, Pallas kernels, on_device(): pl.pallas_call(functools.partial(kernel, sizes), out_shape=(jax.ShapeDtyp...  72.4 us
    concatenate x5, local copies, waits for them, and re-layouts, on_device(): jnp.concatenate([displacements, species.astype(F32)[None], jnp.zeros((4,)...  1.9 us

profile of v1, /device:TPU:1, one launch (start us, length us, event | category | flops | bytes accessed | tf_op | source)
XLA Modules:
  0.0 78.6 jit_solution(11849765268871819181)
XLA Ops:
  0.6 0.0 copy-start.5
  1.3 0.8 concatenate.12
  2.1 0.7 convert_element_type.6
  2.8 0.1 concatenate.13
  2.9 0.9 %concatenate.14 = f32[24,128]{1,0:T(8,128)S(1)} reshape(f32[8,3,2,2,32]{4,3,2,1,0:T(2,128)} %param.13) | data formatting | bytes 24576 | tf_op jit(solution)/shard_map/concatenate | solution.py:597
  3.8 0.0 copy-done.5
  3.8 0.0 copy-start
  3.8 0.1 concatenate.15
  3.9 0.0 copy-start.1
  3.9 0.0 copy-start.2
  3.9 0.0 copy-start.3
  4.0 0.0 copy-start.4
  4.0 0.6 copy-done
  4.6 0.1 copy-done.1
  4.7 0.0 copy-done.2
  4.7 0.0 copy-done.3
  4.7 0.0 copy-done.4
  4.7 72.4 %chebyshev.1 = (f32[2,24,128]{2,1,0:T(8,128)S(1)}, f32[8,128]{1,0:T(8,128)S(1)}) custom-call(f32[1]{0:T(128)S(6)} %copy.13.radius_ref, f32[64,128]{1,0:T(8,128)S(1)} %concatenate.16.pack_ref, f32[3,128]{1,0:T(4,128)S(1)} %copy-done.3, f32[8,64]{1,0:T(8,128)S(1)} %copy-done.2, f32[64,128]{1,0:T(8,128)S(1)} %copy-done.1, f32[128,128]{1,0:T(8,128)S(1)} %copy-done, ...), custom_call_target="tpu_custom_call" | custom-call | tf_op jit(solution)/shard_map/chebyshev/pallas_call | solution.py:609
  77.1 0.7 copy.12
  77.8 0.8 reshape.20
  (4 shorter events, 0.1 us)
Async XLA Ops:
  0.6 3.1 %copy-start.5 = (s32[32,2,2,32]{3,2,1,0:T(2,128)S(1)}, s32[32,2,2,32]{3,2,1,0:T(2,128)}, u32[]{:S(2)}) copy-start(s32[32,2,2,32]{3,2,1,0:T(2,128)} %param.12) | copy-start | bytes 49156
  3.8 0.8 %copy-start = (f32[128,128]{1,0:T(8,128)S(1)}, f32[128,128]{1,0:T(8,128)}, u32[]{:S(2)}) copy-start(f32[128,128]{1,0:T(8,128)} %wn_ref.1) | copy-start | bytes 196612
  3.9 0.8 copy-start.1
  3.9 0.8 copy-start.2
  3.9 0.8 copy-start.3
  4.0 0.7 copy-start.4

commit v2 on v1

v2 whole, which is shorter than its diff:
```python
import functools
import math

import jax
import jax.numpy as jnp
from jax import lax
from jax.experimental import pallas as pl
from jax.experimental.pallas import tpu as pltpu
from jax.sharding import PartitionSpec as P

SPACING = 2.2
CUTOFF = 5.0
NORM_SCALE = 0.22360679774997896
MASSES = (28.0855, 15.999, 22.99)
HIGHEST = lax.Precision.HIGHEST
MESH = pl.DeviceIdType.MESH
F32 = jnp.float32
BF16 = jnp.bfloat16

CODES = tuple(sorted((c for c in range(27) if c != 13), key=lambda c: (c % 3 != 1, c)))
ORDER = {c: n for n, c in enumerate(CODES)}
NC = len(CODES)
FLAT = 8
BLOCKS = ((0, 7), (7, 14), (14, 20), (20, 26))
AXES = ("gx", "gy", "gz")
LANES = 128
HID = 64
PROBES = 8


def roll(value, by):
    return pltpu.roll(value, by % LANES, 1)


def high_low(value):
    high = value.astype(BF16).astype(F32)
    return high, value - high


def by_species(species, values):
    return jnp.where(species < 0.5, values[0], jnp.where(species < 1.5, values[1], values[2]))


def sin_cos(angle):
    off = angle - math.pi / 2
    square = off * off
    odd = jnp.full_like(off, -1.0 / math.factorial(15))
    for power in (13, 11, 9, 7, 5, 3, 1):
        odd = odd * square + (-1.0) ** (power // 2) / math.factorial(power)
    even = jnp.full_like(off, 1.0 / math.factorial(16))
    for power in (14, 12, 10, 8, 6, 4, 2, 0):
        even = even * square + (-1.0) ** (power // 2) / math.factorial(power)
    return even, -odd * off


class Lanes:
    def __init__(self):
        lane = lax.broadcasted_iota(jnp.int32, (8, LANES), 1)
        self.lane = lane
        self.upper = (lane >= 64, (lane & 32) != 0)
        self.z = lane & 31
        self.low_z = self.z < 16
        self.first = [self.z == j for j in range(3)]
        self.last = [self.z == 31 - j for j in range(3)]

    def swap(self, axis, value):
        if axis == 0:
            return roll(value, 64)
        return jnp.where(self.upper[1], roll(value, 32), roll(value, -32))

    def merge(self, axis, low_value, high_value):
        if axis < 2:
            return jnp.where(self.upper[axis], high_value, low_value)
        return jnp.where(self.low_z, low_value, high_value)

    def ends(self, low_values, high_values):
        out = jnp.zeros((8, LANES), F32)
        for j, (low, high) in enumerate(zip(low_values, high_values)):
            out = jnp.where(self.first[j], low, jnp.where(self.last[j], high, out))
        return out

    def pack(self, values):
        return self.ends(
            [roll(v, j) if j else v for j, v in enumerate(values)],
            [roll(v, -j) if j else v for j, v in enumerate(values)],
        )

    def unpack(self, packed, count):
        out = []
        for j in range(count):
            low, high = (roll(packed, -j), roll(packed, j)) if j else (packed, packed)
            out.append(jnp.where(self.first[0], low, jnp.where(self.last[0], high, 0.0)))
        return out


SITES = tuple((gx, gy) for gx in (0, 1) for gy in (0, 1))


def gather(lanes, ext, flat_only=False):
    count = len(ext[0, 0]) - 1
    along_x = {}
    for gy in (0, 1):
        own, ghost = ext[0, gy], ext[1, gy]
        along_x[0, gy] = own
        along_x[1, gy] = [lanes.swap(0, lanes.merge(0, g, o)) for o, g in zip(own, ghost)]
        along_x[-1, gy] = [lanes.swap(0, lanes.merge(0, o, g)) for o, g in zip(own, ghost)]
    out = {}
    for sx in (-1, 0, 1):
        own, ghost = along_x[sx, 0], along_x[sx, 1]
        along_y = {
            0: own,
            1: [lanes.swap(1, lanes.merge(1, g, o)) for o, g in zip(own, ghost)],
            -1: [lanes.swap(1, lanes.merge(1, o, g)) for o, g in zip(own, ghost)],
        }
        for sy in (-1, 0, 1):
            values, packed = along_y[sy][:count], along_y[sy][count]
            base = (sx + 1) * 9 + (sy + 1) * 3 + 1
            out[base] = values
            if flat_only:
                continue
            out[base + 1] = [
                jnp.where(lanes.last[0], roll(packed, 31 - j), roll(v, -1))
                for j, v in enumerate(values)
            ]
            out[base - 1] = [
                jnp.where(lanes.first[0], roll(packed, j - 31), roll(v, 1))
                for j, v in enumerate(values)
            ]
    return out


def scatter(lanes, edges):
    along_z = {}
    for sx in (-1, 0, 1):
        for sy in (-1, 0, 1):
            base = (sx + 1) * 9 + (sy + 1) * 3 + 1
            values, lows, highs = [], [], []
            for j in range(3):
                up, down = edges(base + 1, j), edges(base - 1, j)
                own = edges(base, j)
                own = own + jnp.where(lanes.first[0], 0.0, roll(up, 1))
                values.append(own + jnp.where(lanes.last[0], 0.0, roll(down, -1)))
                lows.append(roll(up, j - 31))
                highs.append(roll(down, 31 - j))
            along_z[sx, sy] = values + [lanes.ends(lows, highs)]
    along_y = {}
    for sx in (-1, 0, 1):
        items = list(zip(along_z[sx, -1], along_z[sx, 0], along_z[sx, 1]))
        along_y[sx, 0] = [m + lanes.swap(1, lanes.merge(1, up, down)) for down, m, up in items]
        along_y[sx, 1] = [lanes.swap(1, lanes.merge(1, down, up)) for down, m, up in items]
    ext = {}
    for gy in (0, 1):
        items = list(zip(along_y[-1, gy], along_y[0, gy], along_y[1, gy]))
        ext[0, gy] = [m + lanes.swap(0, lanes.merge(0, up, down)) for down, m, up in items]
        ext[1, gy] = [lanes.swap(0, lanes.merge(0, down, up)) for down, m, up in items]
    return ext


def kernel(
    sizes,
    radius_ref,
    *refs,
):
    sources, refs = refs[:9], refs[9:]
    (
        cheb_ref,
        result_ref,
        moments_ref,
        geo_send,
        geo_recv,
        halo_send,
        halo_recv,
        fold_send,
        fold_recv,
        sum_send,
        sum_recv,
        geo_sems,
        halo_sems,
        fold_sems,
        sum_sems,
        geo_ref,
        trig_ref,
        rows_ref,
        acc_ref,
        prod_ref,
        second_ref,
        node_ref,
        matrix_ref,
        dv_ref,
        dr_ref,
        edge_ref,
        small_ref,
        pack_ref,
    ) = refs[: -10]
    fetched, fetch_sems = refs[-10:-1], refs[-1]
    disp_ref, species_ref, index_ref, probes_ref, emb_ref, w1_ref, w2_ref, wn_ref, readout_ref = fetched
    fetches = [
        pltpu.make_async_copy(src, dst, fetch_sems.at[n])
        for n, (src, dst) in enumerate(zip(sources, fetched))
    ]
    for n in (0, 1, 3, 4, 5, 6, 7, 8, 2):
        fetches[n].start()

    place = [lax.axis_index(axis) for axis in AXES]

    def partner(axis, by):
        return lax.rem(place[axis] + (by + sizes[axis]), sizes[axis])

    barrier = pltpu.get_barrier_semaphore()
    partners = [(axis, by) for axis in range(3) for by in range(1, sizes[axis])]
    for axis, by in partners:
        pl.semaphore_signal(
            barrier, inc=1, device_id={AXES[axis]: partner(axis, by)}, device_id_type=MESH
        )

    def flat(ref, first, count, stride):
        return jnp.concatenate(
            [ref[pl.ds(first + q, count, stride=stride), :] for q in range(4)], axis=1
        )

    lanes = Lanes()
    pack_ref[0:8, :] = jnp.zeros((8, LANES), F32)
    for n in (0, 1):
        fetches[n].wait()
    pack_ref[0:3, :] = jnp.concatenate([disp_ref[:, q, :] for q in range(4)], axis=1)
    pack_ref[3:4, :] = jnp.concatenate(
        [species_ref[q : q + 1, :] for q in range(4)], axis=1
    ).astype(F32)
    for n in (3,):
        fetches[n].wait()
    species = pack_ref[3:4, :]
    inv_root = by_species(species, [1.0 / math.sqrt(m) for m in MASSES])
    root = by_species(species, [math.sqrt(m) for m in MASSES])
    probes = [flat(probes_ref, 4 * j, PROBES, 12) for j in range(3)]
    start = [p * inv_root for p in probes]

    pl.semaphore_wait(barrier, len(partners))

    def copy(src, dst, sems, number, axis, by):
        return pltpu.make_async_remote_copy(
            src_ref=src,
            dst_ref=dst,
            send_sem=sems.at[0, number],
            recv_sem=sems.at[1, number],
            device_id={AXES[axis]: partner(axis, by)},
            device_id_type=MESH,
        )

    def tile(n):
        return pl.ds(8 * n, 8)

    def halo_start(send, recv, sems, axis, arrays):
        for n, value in enumerate(arrays):
            send[axis, tile(n), :] = value
        rows = pl.ds(0, 8 * len(arrays))
        copies = [
            copy(send.at[axis, rows], recv.at[axis, d, rows], sems, 2 * axis + d, axis, 1 - 2 * d)
            for d in (0, 1)
        ]
        for c in copies:
            c.start()
        return copies

    def halo_finish(recv, axis, copies, count):
        for c in copies:
            c.wait()
        return [
            lanes.merge(axis, recv[axis, 1, tile(n), :], recv[axis, 0, tile(n), :])
            for n in range(count)
        ]

    geometry = {(0, 0): [pack_ref[0:8, :]]}
    geo = (geo_send, geo_recv, geo_sems)
    halo = (halo_send, halo_recv, halo_sems)
    copies = halo_start(*geo, 1, geometry[0, 0])
    halo_copies = halo_start(*halo, 1, start)

    for n in (4, 5, 6, 7, 8, 2):
        fetches[n].wait()
    for s in range(3):
        acc_ref[pl.ds(64 * s, 64), :] = w2_ref[...] * emb_ref[s : s + 1, :]
    to_node = jnp.dot(
        acc_ref[...], wn_ref[...], precision=HIGHEST, preferred_element_type=F32
    ) * NORM_SCALE
    flipped = [jnp.transpose(to_node[64 * s : 64 * s + 64, :]) for s in range(3)]
    flip = [high_low(f) for f in flipped]
    left_node = jnp.concatenate(
        [jnp.concatenate([hi, hi, lo], axis=1) for hi, lo in flip], axis=0
    ).astype(BF16)
    first_high, first_low = high_low(w1_ref[...] * math.sqrt(2.0 / CUTOFF))
    left_radial = jnp.transpose(
        jnp.concatenate([first_high, first_high, first_low, jnp.zeros_like(first_high)], axis=0)
    ).astype(BF16)
    small_ref[0:8, :] = jnp.zeros((8, LANES), F32)
    small_ref[0:3, :] = emb_ref[...]
    small_ref[3:4, :] = readout_ref[...]
    columns = jnp.transpose(small_ref[0:8, :])
    readout = columns[:, 3:4]

    row_lane = lax.broadcasted_iota(jnp.int32, (32, LANES), 1)
    home = (
        ((row_lane >> 6) + 1) * (4 * 34) + (((row_lane >> 5) & 1) + 1) * 34 + (row_lane & 31) + 1
    )
    off = flat(index_ref, 0, 32, 4) - home

    def unit(value, bound):
        return jnp.where(value > bound, 1, 0) - jnp.where(value < -bound, 1, 0)

    off_x = unit(off, 68)
    rest = off - 136 * off_x
    off_y = unit(rest, 17)
    off_z = rest - 34 * off_y
    code = (off_x + 1) * 9 + (off_y + 1) * 3 + off_z + 1
    bits = jnp.where(off == 0, 0, jnp.left_shift(jnp.ones_like(code), code))
    bits = jnp.sum(bits, axis=0, keepdims=True)

    geometry[0, 1] = halo_finish(geo_recv, 1, copies, 1)
    copies = halo_start(*geo, 0, geometry[0, 0] + geometry[0, 1])
    y_old = {(0, 0): start}
    y_old[0, 1] = halo_finish(halo_recv, 1, halo_copies, 3)
    ghosts = halo_finish(geo_recv, 0, copies, 2)
    geometry[1, 0], geometry[1, 1] = [ghosts[0]], [ghosts[1]]
    copies = halo_start(*geo, 2, [geometry[k][0] for k in SITES])
    halo_copies = halo_start(*halo, 0, y_old[0, 0] + y_old[0, 1])

    for n, c in enumerate(CODES):
        rows_ref[9, pl.ds(n, 1), :] = (jnp.right_shift(bits, c) & 1).astype(F32)

    def edges_of(seen, count):
        for n in range(count):
            geo_ref[tile(n), :] = seen[CODES[n]][0]
        code_row = lax.broadcasted_iota(jnp.int32, (count, LANES), 0)
        if count == FLAT:
            number = code_row + jnp.where(code_row >= 4, 1, 0)
            offs = (number // 3, number % 3, jnp.ones_like(number))
        else:
            number = code_row + jnp.where(code_row >= 4, 1, 0)
            pair = (code_row - FLAT) // 2
            flat = code_row < FLAT
            offs = (
                jnp.where(flat, number // 3, pair // 3),
                jnp.where(flat, number % 3, pair % 3),
                jnp.where(flat, 1, 2 * (code_row % 2)),
            )
        vectors = [
            (off - 1).astype(F32) * SPACING
            + geo_ref[pl.ds(j, count, stride=8), :]
            - pack_ref[j : j + 1, :]
            for j, off in enumerate(offs)
        ]
        filled = rows_ref[9, 0:count, :]
        present = filled > 0.5
        square = vectors[0] * vectors[0] + vectors[1] * vectors[1] + vectors[2] * vectors[2]
        distance = jnp.sqrt(jnp.where(present, square, 1.0))
        inverse = 1.0 / distance
        part = distance * (1.0 / CUTOFF)
        part_sq = part * part
        for j in range(3):
            rows_ref[j, 0:count, :] = vectors[j] * inverse
        rows_ref[3, 0:count, :] = inverse
        rows_ref[4, 0:count, :] = filled * (1.0 - part_sq) * (1.0 - part_sq)
        rows_ref[5, 0:count, :] = filled * (-4.0 / CUTOFF) * part * (1.0 - part_sq)
        rows_ref[6, 0:count, :] = filled * (-4.0 / CUTOFF**2) * (1.0 - 3.0 * part_sq)
        rows_ref[7, 0:count, :] = geo_ref[pl.ds(3, count, stride=8), :]
        sin_1, cos_1 = sin_cos(distance * (math.pi / CUTOFF))
        sin_k, cos_k = sin_1, cos_1
        sin_b, cos_b = jnp.zeros_like(sin_1), jnp.ones_like(cos_1)
        for k in range(8):
            omega = (k + 1) * math.pi / CUTOFF
            trig_ref[pl.ds(k, count, stride=24), :] = sin_k
            trig_ref[pl.ds(8 + k, count, stride=24), :] = cos_k * omega
            trig_ref[pl.ds(16 + k, count, stride=24), :] = sin_k * (-omega * omega)
            sin_k, sin_b = 2.0 * cos_1 * sin_k - sin_b, sin_k
            cos_k, cos_b = 2.0 * cos_1 * cos_k - cos_b, cos_k

    edges_of(gather(lanes, {k: v + v for k, v in geometry.items()}, True), FLAT)

    acc_ref[...] = jnp.zeros_like(acc_ref)

    def radial(pair, carry):
        blocks = []
        for i in (0, 1):
            for g in range(3):
                hi, lo = high_low(trig_ref[pl.ds((2 * pair + i) * 24 + 8 * g, 8), :])
                blocks.append(jnp.concatenate([hi, lo, hi, jnp.zeros_like(hi)], axis=0))
        right = jnp.concatenate(blocks, axis=1).astype(BF16)
        waves = jnp.dot(left_radial, right, preferred_element_type=F32)
        rights = []
        for i in (0, 1):
            n = 2 * pair + i
            wave = [waves[:, 128 * (3 * i + g) : 128 * (3 * i + g + 1)] for g in range(3)]
            inv = rows_ref[3, pl.ds(n, 1), :]
            env = [rows_ref[4 + g, pl.ds(n, 1), :] for g in range(3)]
            kind = rows_ref[7, pl.ds(n, 1), :]
            x_0 = wave[0] * inv
            x_1 = (wave[1] - x_0) * inv
            x_2 = (wave[2] - 2.0 * x_1) * inv
            gate = 1.0 / (1.0 + jnp.exp(-x_0))
            shut = 1.0 - gate
            value = x_0 * gate
            slope = gate + value * shut
            bend = shut * (2.0 * gate + value * (1.0 - 2.0 * gate))
            r_1 = slope * x_1
            r_2 = bend * x_1 * x_1 + slope * x_2
            h_0 = value * env[0]
            h_1 = r_1 * env[0] + value * env[1]
            h_2 = r_2 * env[0] + 2.0 * r_1 * env[1] + value * env[2]
            second_ref[n] = h_2
            for s in range(3):
                one = jnp.where(jnp.abs(kind - s) < 0.5, 1.0, 0.0)
                acc_ref[pl.ds(64 * s, 64), :] += h_0 * one
            hi, lo = high_low(h_1)
            rights.append(jnp.concatenate([hi, lo, hi], axis=0).astype(BF16))
        product = jnp.dot(
            left_node, jnp.concatenate(rights, axis=1), preferred_element_type=F32
        )
        for i in (0, 1):
            n = 2 * pair + i
            kind = rows_ref[7, pl.ds(n, 1), :]
            cols = slice(128 * i, 128 * i + 128)
            prod_ref[n] = by_species(
                kind, [product[128 * s : 128 * s + 128, cols] for s in range(3)]
            )
        return carry

    lax.fori_loop(0, FLAT // 2, radial, 0, unroll=True)
    ghosts = halo_finish(geo_recv, 2, copies, 4)
    for n, k in enumerate(SITES):
        geometry[k] = geometry[k] + [ghosts[n]]
    edges_of(gather(lanes, geometry), NC)
    ghosts = halo_finish(halo_recv, 0, halo_copies, 6)
    y_old[1, 0], y_old[1, 1] = ghosts[:3], ghosts[3:]
    halo_copies = halo_start(*halo, 2, [lanes.pack(y_old[k]) for k in SITES])
    lax.fori_loop(FLAT // 2, NC // 2, radial, 0, unroll=True)

    home_kind = jnp.where(
        lax.broadcasted_iota(jnp.int32, (8, LANES), 0).astype(F32) == species, 1.0, 0.0
    )
    home_kind = jnp.where(lax.broadcasted_iota(jnp.int32, (8, LANES), 0) < 3, home_kind, 0.0)
    node = jnp.dot(columns, home_kind, precision=HIGHEST, preferred_element_type=F32)
    node = node + jnp.dot(
        jnp.concatenate(flipped, axis=1), acc_ref[...], precision=HIGHEST, preferred_element_type=F32
    )
    gate = 1.0 / (1.0 + jnp.exp(-node))
    shut = 1.0 - gate
    value = node * gate
    node_slope = readout * (gate + value * shut)
    node_ref[0] = node_slope
    node_ref[1] = readout * (shut * (2.0 * gate + value * (1.0 - 2.0 * gate)))
    acc_ref[...] = jnp.dot(to_node, node_slope, precision=HIGHEST, preferred_element_type=F32)

    def edge_terms(n, carry):
        mine = prod_ref[n]
        kind = rows_ref[7, pl.ds(n, 1), :]
        pull = jnp.sum(mine * node_ref[0], axis=0, keepdims=True) * rows_ref[3, pl.ds(n, 1), :]
        back = by_species(kind, [acc_ref[64 * s : 64 * s + 64, :] for s in range(3)])
        curve = jnp.sum(back * second_ref[n], axis=0, keepdims=True)
        rows_ref[8, pl.ds(n, 1), :] = pull
        rows_ref[10, pl.ds(n, 1), :] = curve - pull
        return carry

    lax.fori_loop(0, NC, edge_terms, 0)
    for low, high in BLOCKS:

        def edge_matrix(n, carry, low=low, high=high):
            bent = prod_ref[n] * node_ref[1]
            for m in range(high):
                both = jnp.sum(bent * prod_ref[m], axis=0, keepdims=True)
                both = jnp.broadcast_to(both, (8, LANES))
                matrix_ref[n * NC + m] = both
                if m < low:
                    matrix_ref[m * NC + n] = both
            matrix_ref[n * NC + n] = matrix_ref[n * NC + n] + rows_ref[10, pl.ds(n, 1), :]
            return carry

        lax.fori_loop(low, high, edge_matrix, 0)

    ghosts = halo_finish(halo_recv, 2, halo_copies, 4)
    for n, k in enumerate(SITES):
        y_old[k] = y_old[k] + [ghosts[n]]
    scale = 1.0 / radius_ref[0]
    weight_sq = {}
    for k in SITES:
        own, ghost = [
            by_species(g[3:4, :], [1.0 / m for m in MASSES]) * scale + jnp.zeros((8, LANES), F32)
            for g in geometry[k]
        ]
        weight_sq[k] = [own] * 3 + [lanes.pack([ghost] * 3)]

    def local_product(y):
        views = gather(lanes, y)
        for n, c in enumerate(CODES):
            total = jnp.zeros((8, LANES), F32)
            for j in range(3):
                change = views[c][j] - views[13][j]
                dv_ref[3 * n + j] = change
                total = total + rows_ref[j, n : n + 1, :] * change
            dr_ref[n] = total

        def force(n, carry):
            total = matrix_ref[n * NC] * dr_ref[0]
            for m in range(1, NC):
                total = total + matrix_ref[n * NC + m] * dr_ref[m]
            pull = rows_ref[8, pl.ds(n, 1), :]
            out, work = [], carry[3]
            for j in range(3):
                change = dv_ref[3 * n + j]
                edge = rows_ref[j, pl.ds(n, 1), :] * total + pull * change
                edge_ref[3 * n + j] = edge
                out.append(carry[j] - edge)
                work = work + edge * change
            return tuple(out) + (work,)

        zero = jnp.zeros((8, LANES), F32)
        centre = lax.fori_loop(0, NC, force, (zero,) * 4, unroll=2)
        terms = scatter(
            lanes, lambda c, j: centre[j] if c == 13 else edge_ref[3 * ORDER[c] + j]
        )
        return terms, centre[3] * scale

    def exchange(number, held, own_only, beside):
        for axis in (1, 0, 2):
            if axis < 2:
                owns = [k for k in SITES if k in held and k[axis] == 0]
                others = [(1, k[1]) if axis == 0 else (k[0], 1) for k in owns]
                own = [v for k in owns for v in held[k]]
                ghost = [v for k in others for v in held[k]]
            else:
                owns = [k for k in SITES if k in held]
                own = [lanes.pack(held[k][:3]) for k in owns]
                ghost = [held[k][3] for k in owns]
            for n in range(len(own)):
                fold_send[number, axis, 0, tile(n), :] = lanes.merge(axis, ghost[n], own[n])
                fold_send[number, axis, 1, tile(n), :] = lanes.merge(axis, own[n], ghost[n])
            rows = pl.ds(0, 8 * len(own))
            copies = [
                copy(
                    fold_send.at[number, axis, d, rows],
                    fold_recv.at[number, axis, d, rows],
                    fold_sems.at[number],
                    2 * axis + d,
                    axis,
                    1 - 2 * d,
                )
                for d in (0, 1)
            ]
            for c in copies:
                c.start()
            beside(axis)
            for c in copies:
                c.wait()
            below = [fold_recv[number, axis, 0, tile(n), :] for n in range(len(own))]
            above = [fold_recv[number, axis, 1, tile(n), :] for n in range(len(own))]
            to_own = [lanes.merge(axis, b, a) for b, a in zip(below, above)]
            to_ghost = [lanes.merge(axis, a, b) for b, a in zip(below, above)]
            after = {}
            for n, key in enumerate(owns):
                if axis < 2:
                    part = slice(4 * n, 4 * n + 4)
                    after[key] = [h + t for h, t in zip(held[key], to_own[part])]
                    if not own_only:
                        other = others[n]
                        after[other] = [h + t for h, t in zip(held[other], to_ghost[part])]
                else:
                    more = lanes.unpack(to_own[n], 3)
                    after[key] = [h + t for h, t in zip(held[key][:3], more)]
                    after[key].append(held[key][3] + to_ghost[n])
            held = after
        return held

    def sum_start(axis):
        sum_send[axis] = moments_ref[...]
        copies = []
        for by in range(1, sizes[axis]):
            c = copy(
                sum_send.at[axis],
                sum_recv.at[axis, by],
                sum_sems.at[axis],
                by,
                axis,
                by,
            )
            c.start()
            copies.append(c)
        return copies

    def sum_finish(axis, copies):
        for c in copies:
            c.wait()
        sum_recv[axis, 0] = sum_send[axis]
        total = jnp.zeros((8, LANES), F32)
        for index in range(sizes[axis]):
            slot = lax.rem(place[axis] + (sizes[axis] - index), sizes[axis])
            total = total + sum_recv[axis, slot]
        moments_ref[...] = total

    terms, work_1 = local_product(y_old)
    product = exchange(0, terms, False, lambda axis: None)
    y_1 = {k: [a * w for a, w in zip(product[k], weight_sq[k])] for k in SITES}
    t_1 = [y_1[0, 0][j] * root for j in range(3)]
    flight = {}

    def beside_second(axis):
        if axis == 1:
            square = sum(p * p for p in probes)
            parts = (
                square,
                work_1,
                2.0 * sum(t * t for t in t_1) - square,
                4.0 * work_2 - 3.0 * work_1,
            )
            packed = jnp.zeros((8, LANES), F32)
            for k in range(4):
                total = jnp.sum(parts[k], axis=1, keepdims=True)
                packed = jnp.where(lanes.lane == k, total, packed)
            moments_ref[...] = packed
            flight[0] = sum_start(0)
        if axis == 2:
            sum_finish(0, flight.pop(0))
            flight[1] = sum_start(1)

    terms, work_2 = local_product(y_1)
    product = exchange(1, terms, False, beside_second)
    y_2 = {
        k: [2.0 * a * w - o for a, w, o in zip(product[k], weight_sq[k], y_old[k])] for k in SITES
    }
    terms, unused = local_product(y_2)

    def spread(which, j, value):
        for q in range(4):
            part = value if q == 0 else roll(value, -32 * q)
            cheb_ref[pl.ds(96 * which + 4 * j + q, PROBES, stride=12), :] = part[:, 0:32]

    def beside_third(axis):
        if axis == 1:
            for j in range(3):
                spread(0, j, y_2[0, 0][j] * root)
            sum_finish(1, flight.pop(1))
            flight[2] = sum_start(2)

    product = exchange(2, terms, True, beside_third)
    for j in range(3):
        spread(1, j, 2.0 * product[0, 0][j] * weight_sq[0, 0][j] * root - t_1[j])
    sum_finish(2, flight.pop(2))
    result_ref[...] = jnp.transpose(moments_ref[...])[0:4, :]


def on_device(
    sizes,
    displacements,
    species,
    neighbor_index,
    probes,
    embedding,
    w_radial1,
    w_radial2,
    w_node,
    readout,
    spectral_radius,
):
    vmem = pl.BlockSpec(memory_space=pltpu.VMEM)
    most = max(sizes)
    operands = (
        displacements.reshape(3, 4, 32),
        species.reshape(-1, 32),
        neighbor_index.reshape(-1, 32),
        probes.reshape(-1, 32),
        embedding,
        w_radial1,
        w_radial2,
        w_node,
        readout.reshape(1, -1),
    )
    cheb, result = pl.pallas_call(
        functools.partial(kernel, sizes),
        out_shape=(
            jax.ShapeDtypeStruct((24 * PROBES, 32), F32),
            jax.ShapeDtypeStruct((4, PROBES), F32),
        ),
        in_specs=[pl.BlockSpec(memory_space=pltpu.SMEM)] + [pl.BlockSpec(memory_space=pl.ANY)] * 9,
        out_specs=(vmem, vmem),
        scratch_shapes=[
            pltpu.VMEM((8, LANES), F32),
            pltpu.VMEM((3, 32, LANES), F32),
            pltpu.VMEM((3, 2, 32, LANES), F32),
            pltpu.VMEM((3, 48, LANES), F32),
            pltpu.VMEM((3, 2, 48, LANES), F32),
            pltpu.VMEM((3, 3, 2, 64, LANES), F32),
            pltpu.VMEM((3, 3, 2, 64, LANES), F32),
            pltpu.VMEM((3, 8, LANES), F32),
            pltpu.VMEM((3, most, 8, LANES), F32),
            pltpu.SemaphoreType.DMA((2, 6)),
            pltpu.SemaphoreType.DMA((2, 6)),
            pltpu.SemaphoreType.DMA((3, 2, 6)),
            pltpu.SemaphoreType.DMA((3, 2, most)),
            pltpu.VMEM((8 * NC, LANES), F32),
            pltpu.VMEM((24 * NC, LANES), F32),
            pltpu.VMEM((11, 32, LANES), F32),
            pltpu.VMEM((3 * HID, LANES), F32),
            pltpu.VMEM((NC, 128, LANES), F32),
            pltpu.VMEM((NC, HID, LANES), F32),
            pltpu.VMEM((2, 128, LANES), F32),
            pltpu.VMEM((NC * NC, 8, LANES), F32),
            pltpu.VMEM((3 * NC, 8, LANES), F32),
            pltpu.VMEM((NC, 8, LANES), F32),
            pltpu.VMEM((3 * NC, 8, LANES), F32),
            pltpu.VMEM((8, LANES), F32),
            pltpu.VMEM((8, LANES), F32),
        ]
        + [pltpu.VMEM(v.shape, v.dtype) for v in operands]
        + [pltpu.SemaphoreType.DMA((len(operands),))],
        compiler_params=pltpu.CompilerParams(
            collective_id=0, has_side_effects=True, vmem_limit_bytes=60 * 2**20
        ),
        name="chebyshev",
    )(
        spectral_radius,
        *operands,
    )
    return cheb.reshape((2,) + probes.shape), result


def solution(mesh):
    placed = (
        P(None, "gx", "gy", "gz"),
        P("gx", "gy", "gz"),
        P(None, "gx", "gy", "gz"),
        P(None, None, "gx", "gy", "gz"),
        P(),
        P(),
        P(),
        P(),
        P(),
        P(),
    )
    return jax.shard_map(
        functools.partial(on_device, tuple(mesh.shape[axis] for axis in AXES)),
        mesh=mesh,
        in_specs=placed,
        out_specs=(P(None, None, None, "gx", "gy", "gz"), P()),
        check_vma=False,
    )
```

time: 78.8 us -> 63.8 us (0.81)
  Pallas kernels: 72.4 us -> 59.5 us
  local copies, waits for them, and re-layouts: 4.06 us -> 2.13 us
    pallas_call x1, Pallas kernels: 72.4 us -> 59.5 us  [on_device(): pl.pallas_call(functools.partial(kernel, sizes), out_shape=(jax.ShapeDtyp...]
    concatenate x5 -> x0, local copies, waits for them, and re-layouts: 1.9 us -> none  [on_device(): jnp.concatenate([displacements, species.astype(F32)[None], jnp.zeros((4,)...]
    unnamed x13 -> x4, local copies, waits for them, and re-layouts: 1.38 us -> 2.13 us
where the time goes in v2:
time: 63.8 us; the launch traced here: 63 us
  Pallas kernels  59.5 us (93%)
  local copies, waits for them, and re-layouts  2.13 us (3%)
  between operations  1.3 us (2%)
    pallas_call x1, Pallas kernels, on_device(): pl.pallas_call(functools.partial(kernel, sizes), out_shape=(jax.ShapeDtyp...  59.5 us
    unnamed x4, local copies, waits for them, and re-layouts  2.13 us

profile of v2, /device:TPU:1, one launch (start us, length us, event | category | flops | bytes accessed | tf_op | source)
XLA Modules:
  0.0 63.0 jit_solution(4691612168571312727)
XLA Ops:
  1.3 59.5 %chebyshev.1 = (f32[192,32]{1,0:T(8,128)}, f32[4,8]{1,0:T(4,128)}) custom-call(f32[1]{0:T(128)S(6)} %copy.14.radius_ref, f32[3,4,32]{2,1,0:T(4,128)} %bitcast.9, s32[4,32]{1,0:T(4,128)} %bitcast.10, s32[128,32]{1,0:T(8,128)} %bitcast.7, f32[96,32]{1,0:T(8,128)} %bitcast.8, f32[3,128]{1,0:T(4,128)} %refs_4_.1, f32[8,64]{1,0:T(8,128)} %refs_5_.1, ...), custom_call_target="tpu_custom_call" | custom-call | tf_op jit(solution)/shard_map/chebyshev/pallas_call | solution.py:674
  60.8 0.0 copy-start
  60.8 1.5 %copy.15 = f32[2,8,3,2,2,32]{5,4,3,2,1,0:T(2,128)} copy(f32[2,8,3,2,2,32]{5,4,3,2,1,0:T(2,128)} %bitcast.6) | data formatting | bytes 49152
  62.4 0.0 copy-done
  62.4 0.6 copy.16
Async XLA Ops:
  60.8 1.6 %copy-start = (f32[4,8]{1,0:T(4,128)S(1)}, f32[4,8]{1,0:T(4,128)}, u32[]{:S(2)}) copy-start(f32[4,8]{1,0:T(4,128)} %get-tuple-element.9) | copy-start | bytes 388

commit v3 on v2

--- a/solution.py
+++ b/solution.py
@@ -21,6 +21,18 @@
 ORDER = {c: n for n, c in enumerate(CODES)}
 NC = len(CODES)
 FLAT = 8
+WAYS = tuple(
+    sorted(
+        (
+            (x, y, z)
+            for x in (-1, 0, 1)
+            for y in (-1, 0, 1)
+            for z in (-1, 0, 1)
+            if (x, y, z) != (0, 0, 0)
+        ),
+        key=lambda way: (way[2] == 0, -sum(map(abs, way))),
+    )
+)
 BLOCKS = ((0, 7), (7, 14), (14, 20), (20, 26))
 AXES = ("gx", "gy", "gz")
 LANES = 128
@@ -60,6 +72,7 @@
         self.upper = (lane >= 64, (lane & 32) != 0)
         self.z = lane & 31
         self.low_z = self.z < 16
+        self.outer = (self.z < 3) | (self.z > 28)
         self.first = [self.z == j for j in range(3)]
         self.last = [self.z == 31 - j for j in range(3)]
 
@@ -519,54 +532,111 @@
         return terms, centre[3] * scale
 
     def exchange(number, held, own_only, beside):
-        for axis in (1, 0, 2):
-            if axis < 2:
-                owns = [k for k in SITES if k in held and k[axis] == 0]
-                others = [(1, k[1]) if axis == 0 else (k[0], 1) for k in owns]
-                own = [v for k in owns for v in held[k]]
-                ghost = [v for k in others for v in held[k]]
+        count = 3 if own_only else 4
+
+        def leaving(axis, sign, table):
+            out = {}
+            for k, own in table.items():
+                if sign == 0:
+                    if k[axis] == 0 or not own_only:
+                        out[k] = own
+                elif k[axis] == 0:
+                    ghost = table[(1, k[1]) if axis == 0 else (k[0], 1)]
+                    pairs = zip(ghost, own) if sign > 0 else zip(own, ghost)
+                    out[k] = [lanes.merge(axis, low, high) for low, high in pairs]
+            return out
+
+        def arriving(axis, plus, minus):
+            out = {}
+            for k in plus:
+                out[k] = [lanes.merge(axis, p, m) for p, m in zip(plus[k], minus[k])]
+                if not own_only:
+                    other = (1, k[1]) if axis == 0 else (k[0], 1)
+                    out[other] = [lanes.merge(axis, m, p) for p, m in zip(plus[k], minus[k])]
+            return out
+
+        def joined(first, *others):
+            return {
+                k: [sum(o[k][n] for o in others) + v for n, v in enumerate(items)]
+                for k, items in first.items()
+            }
+
+        def pair(first, second):
+            moved = lanes.merge(2, roll(second, 3), roll(second, -3))
+            return jnp.where(lanes.outer, first, moved)
+
+        def second_of(both):
+            return lanes.merge(2, roll(both, -3), roll(both, 3))
+
+        layers = {0: {k: v[:count] for k, v in held.items()}}
+        for sign in (1, -1):
+            layers[sign] = {}
+            for k, v in held.items():
+                own = lanes.pack(v[:3])
+                low, high = (v[3], own) if sign > 0 else (own, v[3])
+                layers[sign][k] = [lanes.merge(2, low, high)]
+
+        copies, keys = {}, {}
+        for slot, way in enumerate(WAYS):
+            table = leaving(1, way[1], leaving(0, way[0], layers[way[2]]))
+            keys[way] = sorted(table)
+            items = [v for k in keys[way] for v in table[k]]
+            if way[2] and len(items) > 1:
+                items = [pair(*items[n : n + 2]) for n in range(0, len(items), 2)]
+            for n, v in enumerate(items):
+                fold_send[number, slot, tile(n), :] = v
+            rows = pl.ds(0, 8 * len(items))
+            copies[way] = pltpu.make_async_remote_copy(
+                src_ref=fold_send.at[number, slot, rows],
+                dst_ref=fold_recv.at[number, slot, rows],
+                send_sem=fold_sems.at[number, 0, slot],
+                recv_sem=fold_sems.at[number, 1, slot],
+                device_id=tuple(partner(axis, way[axis]) for axis in range(3)),
+                device_id_type=MESH,
+            )
+            copies[way].start()
+        beside()
+
+        def arrived(*way):
+            slot = WAYS.index(way)
+            copies[way].wait_recv()
+            count_of = count if way[2] == 0 else 1
+            total = count_of * len(keys[way])
+            if way[2] and total > 1:
+                items = []
+                for n in range(total // 2):
+                    both = fold_recv[number, slot, tile(n), :]
+                    items += [both, second_of(both)]
             else:
-                owns = [k for k in SITES if k in held]
-                own = [lanes.pack(held[k][:3]) for k in owns]
-                ghost = [held[k][3] for k in owns]
-            for n in range(len(own)):
-                fold_send[number, axis, 0, tile(n), :] = lanes.merge(axis, ghost[n], own[n])
-                fold_send[number, axis, 1, tile(n), :] = lanes.merge(axis, own[n], ghost[n])
-            rows = pl.ds(0, 8 * len(own))
-            copies = [
-                copy(
-                    fold_send.at[number, axis, d, rows],
-                    fold_recv.at[number, axis, d, rows],
-                    fold_sems.at[number],
-                    2 * axis + d,
-                    axis,
-                    1 - 2 * d,
+                items = [fold_recv[number, slot, tile(n), :] for n in range(total)]
+            return {
+                k: items[count_of * n : count_of * n + count_of] for n, k in enumerate(keys[way])
+            }
+
+        def plane(layer, centre):
+            along_x = arriving(0, arrived(1, 0, layer), arrived(-1, 0, layer))
+            sides = [
+                joined(
+                    arrived(0, s, layer),
+                    arriving(0, arrived(1, s, layer), arrived(-1, s, layer)),
                 )
-                for d in (0, 1)
+                for s in (1, -1)
             ]
-            for c in copies:
-                c.start()
-            beside(axis)
-            for c in copies:
-                c.wait()
-            below = [fold_recv[number, axis, 0, tile(n), :] for n in range(len(own))]
-            above = [fold_recv[number, axis, 1, tile(n), :] for n in range(len(own))]
-            to_own = [lanes.merge(axis, b, a) for b, a in zip(below, above)]
-            to_ghost = [lanes.merge(axis, a, b) for b, a in zip(below, above)]
-            after = {}
-            for n, key in enumerate(owns):
-                if axis < 2:
-                    part = slice(4 * n, 4 * n + 4)
-                    after[key] = [h + t for h, t in zip(held[key], to_own[part])]
-                    if not own_only:
-                        other = others[n]
-                        after[other] = [h + t for h, t in zip(held[other], to_ghost[part])]
-                else:
-                    more = lanes.unpack(to_own[n], 3)
-                    after[key] = [h + t for h, t in zip(held[key][:3], more)]
-                    after[key].append(held[key][3] + to_ghost[n])
-            held = after
-        return held
+            return joined(centre, along_x, arriving(1, *sides))
+
+        sites = SITES[:1] if own_only else SITES
+        flat = plane(0, {k: layers[0][k] for k in sites})
+        above = plane(1, arrived(0, 0, 1))
+        below = plane(-1, arrived(0, 0, -1))
+        out = {}
+        for k in sites:
+            more = lanes.unpack(lanes.merge(2, above[k][0], below[k][0]), 3)
+            out[k] = [h + t for h, t in zip(flat[k][:3], more)]
+            if not own_only:
+                out[k].append(flat[k][3] + lanes.merge(2, below[k][0], above[k][0]))
+        for c in copies.values():
+            c.wait_send()
+        return out
 
     def sum_start(axis):
         sum_send[axis] = moments_ref[...]
@@ -595,35 +665,33 @@
         moments_ref[...] = total
 
     terms, work_1 = local_product(y_old)
-    product = exchange(0, terms, False, lambda axis: None)
+    product = exchange(0, terms, False, lambda: None)
     y_1 = {k: [a * w for a, w in zip(product[k], weight_sq[k])] for k in SITES}
     t_1 = [y_1[0, 0][j] * root for j in range(3)]
     flight = {}
 
-    def beside_second(axis):
-        if axis == 1:
-            square = sum(p * p for p in probes)
-            parts = (
-                square,
-                work_1,
-                2.0 * sum(t * t for t in t_1) - square,
-                4.0 * work_2 - 3.0 * work_1,
-            )
-            packed = jnp.zeros((8, LANES), F32)
-            for k in range(4):
-                total = jnp.sum(parts[k], axis=1, keepdims=True)
-                packed = jnp.where(lanes.lane == k, total, packed)
-            moments_ref[...] = packed
-            flight[0] = sum_start(0)
-        if axis == 2:
-            sum_finish(0, flight.pop(0))
-            flight[1] = sum_start(1)
+    def beside_second():
+        square = sum(p * p for p in probes)
+        parts = (
+            square,
+            work_1,
+            2.0 * sum(t * t for t in t_1) - square,
+            4.0 * work_2 - 3.0 * work_1,
+        )
+        packed = jnp.zeros((8, LANES), F32)
+        for k in range(4):
+            total = jnp.sum(parts[k], axis=1, keepdims=True)
+            packed = jnp.where(lanes.lane == k, total, packed)
+        moments_ref[...] = packed
+        flight[0] = sum_start(0)
 
     terms, work_2 = local_product(y_1)
     product = exchange(1, terms, False, beside_second)
     y_2 = {
         k: [2.0 * a * w - o for a, w, o in zip(product[k], weight_sq[k], y_old[k])] for k in SITES
     }
+    sum_finish(0, flight.pop(0))
+    flight[1] = sum_start(1)
     terms, unused = local_product(y_2)
 
     def spread(which, j, value):
@@ -631,12 +699,11 @@
             part = value if q == 0 else roll(value, -32 * q)
             cheb_ref[pl.ds(96 * which + 4 * j + q, PROBES, stride=12), :] = part[:, 0:32]
 
-    def beside_third(axis):
-        if axis == 1:
-            for j in range(3):
-                spread(0, j, y_2[0, 0][j] * root)
-            sum_finish(1, flight.pop(1))
-            flight[2] = sum_start(2)
+    def beside_third():
+        for j in range(3):
+            spread(0, j, y_2[0, 0][j] * root)
+        sum_finish(1, flight.pop(1))
+        flight[2] = sum_start(2)
 
     product = exchange(2, terms, True, beside_third)
     for j in range(3):
@@ -685,13 +752,13 @@
             pltpu.VMEM((3, 2, 32, LANES), F32),
             pltpu.VMEM((3, 48, LANES), F32),
             pltpu.VMEM((3, 2, 48, LANES), F32),
-            pltpu.VMEM((3, 3, 2, 64, LANES), F32),
-            pltpu.VMEM((3, 3, 2, 64, LANES), F32),
+            pltpu.VMEM((3, 26, 64, LANES), F32),
+            pltpu.VMEM((3, 26, 64, LANES), F32),
             pltpu.VMEM((3, 8, LANES), F32),
             pltpu.VMEM((3, most, 8, LANES), F32),
             pltpu.SemaphoreType.DMA((2, 6)),
             pltpu.SemaphoreType.DMA((2, 6)),
-            pltpu.SemaphoreType.DMA((3, 2, 6)),
+            pltpu.SemaphoreType.DMA((3, 2, 26)),
             pltpu.SemaphoreType.DMA((3, 2, most)),
             pltpu.VMEM((8 * NC, LANES), F32),
             pltpu.VMEM((24 * NC, LANES), F32),

time: 63.8 us -> 56.6 us (0.89); the launches traced: 63 us -> 56.4 us
  Pallas kernels: 59.5 us -> 53 us
    pallas_call x1, Pallas kernels: 59.5 us -> 53 us  [on_device(): pl.pallas_call(functools.partial(kernel, sizes), out_shape=(jax.ShapeDtyp...]
where the time goes in v3:
time: 56.6 us; the launch traced here: 56.4 us
  Pallas kernels  53 us (94%)
  local copies, waits for them, and re-layouts  2.13 us (4%)
  between operations  1.3 us (2%)
    pallas_call x1, Pallas kernels, on_device(): pl.pallas_call(functools.partial(kernel, sizes), out_shape=(jax.ShapeDtyp...  53 us
    unnamed x4, local copies, waits for them, and re-layouts  2.13 us

profile of v3, /device:TPU:1, one launch (start us, length us, event | category | flops | bytes accessed | tf_op | source)
XLA Modules:
  0.0 56.4 jit_solution(7230550038850491057)
XLA Ops:
  1.3 53.0 %chebyshev.1 = (f32[192,32]{1,0:T(8,128)}, f32[4,8]{1,0:T(4,128)}) custom-call(f32[1]{0:T(128)S(6)} %copy.14.radius_ref, f32[3,4,32]{2,1,0:T(4,128)} %bitcast.9, s32[4,32]{1,0:T(4,128)} %bitcast.10, s32[128,32]{1,0:T(8,128)} %bitcast.7, f32[96,32]{1,0:T(8,128)} %bitcast.8, f32[3,128]{1,0:T(4,128)} %refs_4_.1, f32[8,64]{1,0:T(8,128)} %refs_5_.1, ...), custom_call_target="tpu_custom_call" | custom-call | tf_op jit(solution)/shard_map/chebyshev/pallas_call | solution.py:741
  54.3 0.0 copy-start
  54.3 1.5 %copy.15 = f32[2,8,3,2,2,32]{5,4,3,2,1,0:T(2,128)} copy(f32[2,8,3,2,2,32]{5,4,3,2,1,0:T(2,128)} %bitcast.6) | data formatting | bytes 49152
  55.8 0.0 copy-done
  55.8 0.6 %copy.16 = f32[4,8]{1,0:T(4,128)} copy(f32[4,8]{1,0:T(4,128)S(1)} %copy-done) | data formatting | bytes 256
Async XLA Ops:
  54.3 1.6 %copy-start = (f32[4,8]{1,0:T(4,128)S(1)}, f32[4,8]{1,0:T(4,128)}, u32[]{:S(2)}) copy-start(f32[4,8]{1,0:T(4,128)} %get-tuple-element.9) | copy-start | bytes 388

commit v4 on v3

--- a/solution.py
+++ b/solution.py
@@ -203,6 +203,8 @@
         dr_ref,
         edge_ref,
         small_ref,
+        node_change_ref,
+        total_ref,
         pack_ref,
     ) = refs[: -10]
     fetched, fetch_sems = refs[-10:-1], refs[-1]
@@ -472,21 +474,22 @@
         rows_ref[10, pl.ds(n, 1), :] = curve - pull
         return carry
 
-    lax.fori_loop(0, NC, edge_terms, 0)
-    for low, high in BLOCKS:
-
-        def edge_matrix(n, carry, low=low, high=high):
-            bent = prod_ref[n] * node_ref[1]
-            for m in range(high):
-                both = jnp.sum(bent * prod_ref[m], axis=0, keepdims=True)
-                both = jnp.broadcast_to(both, (8, LANES))
-                matrix_ref[n * NC + m] = both
-                if m < low:
-                    matrix_ref[m * NC + n] = both
-            matrix_ref[n * NC + n] = matrix_ref[n * NC + n] + rows_ref[10, pl.ds(n, 1), :]
-            return carry
-
-        lax.fori_loop(low, high, edge_matrix, 0)
+    lax.fori_loop(0, NC, edge_terms, 0, unroll=2)
+    def matrices():
+        for low, high in BLOCKS:
+
+            def edge_matrix(n, carry, low=low, high=high):
+                bent = prod_ref[n] * node_ref[1]
+                for m in range(high):
+                    both = jnp.sum(bent * prod_ref[m], axis=0, keepdims=True)
+                    both = jnp.broadcast_to(both, (8, LANES))
+                    matrix_ref[n * NC + m] = both
+                    if m < low:
+                        matrix_ref[m * NC + n] = both
+                matrix_ref[n * NC + n] = matrix_ref[n * NC + n] + rows_ref[10, pl.ds(n, 1), :]
+                return carry
+
+            lax.fori_loop(low, high, edge_matrix, 0)
 
     ghosts = halo_finish(halo_recv, 2, halo_copies, 4)
     for n, k in enumerate(SITES):
@@ -500,7 +503,7 @@
         ]
         weight_sq[k] = [own] * 3 + [lanes.pack([ghost] * 3)]
 
-    def local_product(y):
+    def local_product(y, through_node=False):
         views = gather(lanes, y)
         for n, c in enumerate(CODES):
             total = jnp.zeros((8, LANES), F32)
@@ -510,10 +513,28 @@
                 total = total + rows_ref[j, n : n + 1, :] * change
             dr_ref[n] = total
 
+        if through_node:
+            def one_probe(p, carry):
+                for part in range(2):
+                    half = pl.ds(64 * part, 64)
+                    change = jnp.zeros((64, LANES), F32)
+                    for n in range(NC):
+                        change = change + prod_ref[n, half, :] * dr_ref[n, pl.ds(p, 1), :]
+                    node_change_ref[half, :] = change * node_ref[1, half, :]
+                for n in range(NC):
+                    both = jnp.sum(prod_ref[n] * node_change_ref[...], axis=0, keepdims=True)
+                    total_ref[n, pl.ds(p, 1), :] = both
+                return carry
+
+            lax.fori_loop(0, PROBES, one_probe, 0)
+
         def force(n, carry):
-            total = matrix_ref[n * NC] * dr_ref[0]
-            for m in range(1, NC):
-                total = total + matrix_ref[n * NC + m] * dr_ref[m]
+            if through_node:
+                total = total_ref[n] + rows_ref[10, pl.ds(n, 1), :] * dr_ref[n]
+            else:
+                total = matrix_ref[n * NC] * dr_ref[0]
+                for m in range(1, NC):
+                    total = total + matrix_ref[n * NC + m] * dr_ref[m]
             pull = rows_ref[8, pl.ds(n, 1), :]
             out, work = [], carry[3]
             for j in range(3):
@@ -664,8 +685,8 @@
             total = total + sum_recv[axis, slot]
         moments_ref[...] = total
 
-    terms, work_1 = local_product(y_old)
-    product = exchange(0, terms, False, lambda: None)
+    terms, work_1 = local_product(y_old, True)
+    product = exchange(0, terms, False, matrices)
     y_1 = {k: [a * w for a, w in zip(product[k], weight_sq[k])] for k in SITES}
     t_1 = [y_1[0, 0][j] * root for j in range(3)]
     flight = {}
@@ -772,6 +793,8 @@
             pltpu.VMEM((NC, 8, LANES), F32),
             pltpu.VMEM((3 * NC, 8, LANES), F32),
             pltpu.VMEM((8, LANES), F32),
+            pltpu.VMEM((128, LANES), F32),
+            pltpu.VMEM((NC, 8, LANES), F32),
             pltpu.VMEM((8, LANES), F32),
         ]
         + [pltpu.VMEM(v.shape, v.dtype) for v in operands]

time: 56.6 us -> 55.4 us (0.979)
  Pallas kernels: 53 us -> 51.8 us
    pallas_call x1, Pallas kernels: 53 us -> 51.8 us  [on_device(): pl.pallas_call(functools.partial(kernel, sizes), out_shape=(jax.ShapeDtyp...]
where the time goes in v4:
time: 55.4 us; the launch traced here: 55.3 us
  Pallas kernels  51.8 us (94%)
  local copies, waits for them, and re-layouts  2.13 us (4%)
  between operations  1.3 us (2%)
    pallas_call x1, Pallas kernels, on_device(): pl.pallas_call(functools.partial(kernel, sizes), out_shape=(jax.ShapeDtyp...  51.8 us
    unnamed x4, local copies, waits for them, and re-layouts  2.13 us

profile of v4, /device:TPU:1, one launch (start us, length us, event | category | flops | bytes accessed | tf_op | source)
XLA Modules:
  0.0 55.3 jit_solution(1753959727576577980)
XLA Ops:
  1.3 51.8 %chebyshev.1 = (f32[192,32]{1,0:T(8,128)}, f32[4,8]{1,0:T(4,128)}) custom-call(f32[1]{0:T(128)S(6)} %copy.14.radius_ref, f32[3,4,32]{2,1,0:T(4,128)} %bitcast.9, s32[4,32]{1,0:T(4,128)} %bitcast.10, s32[128,32]{1,0:T(8,128)} %bitcast.7, f32[96,32]{1,0:T(8,128)} %bitcast.8, f32[3,128]{1,0:T(4,128)} %refs_4_.1, f32[8,64]{1,0:T(8,128)} %refs_5_.1, ...), custom_call_target="tpu_custom_call" | custom-call | tf_op jit(solution)/shard_map/chebyshev/pallas_call | solution.py:762
  53.1 0.0 copy-start
  53.1 1.5 %copy.15 = f32[2,8,3,2,2,32]{5,4,3,2,1,0:T(2,128)} copy(f32[2,8,3,2,2,32]{5,4,3,2,1,0:T(2,128)} %bitcast.6) | data formatting | bytes 49152
  54.7 0.0 copy-done
  54.7 0.6 %copy.16 = f32[4,8]{1,0:T(4,128)} copy(f32[4,8]{1,0:T(4,128)S(1)} %copy-done) | data formatting | bytes 256
Async XLA Ops:
  53.1 1.6 %copy-start = (f32[4,8]{1,0:T(4,128)S(1)}, f32[4,8]{1,0:T(4,128)}, u32[]{:S(2)}) copy-start(f32[4,8]{1,0:T(4,128)} %get-tuple-element.9) | copy-start | bytes 388

commit v5 on v4

--- a/solution.py
+++ b/solution.py
@@ -514,19 +514,24 @@
             dr_ref[n] = total
 
         if through_node:
-            def one_probe(p, carry):
+            def two_probes(step, carry):
                 for part in range(2):
                     half = pl.ds(64 * part, 64)
-                    change = jnp.zeros((64, LANES), F32)
+                    change = [jnp.zeros((64, LANES), F32) for i in (0, 1)]
                     for n in range(NC):
-                        change = change + prod_ref[n, half, :] * dr_ref[n, pl.ds(p, 1), :]
-                    node_change_ref[half, :] = change * node_ref[1, half, :]
+                        mine = prod_ref[n, half, :]
+                        for i in (0, 1):
+                            change[i] = change[i] + mine * dr_ref[n, pl.ds(2 * step + i, 1), :]
+                    for i in (0, 1):
+                        node_change_ref[i, half, :] = change[i] * node_ref[1, half, :]
                 for n in range(NC):
-                    both = jnp.sum(prod_ref[n] * node_change_ref[...], axis=0, keepdims=True)
-                    total_ref[n, pl.ds(p, 1), :] = both
+                    mine = prod_ref[n]
+                    for i in (0, 1):
+                        both = jnp.sum(mine * node_change_ref[i], axis=0, keepdims=True)
+                        total_ref[n, pl.ds(2 * step + i, 1), :] = both
                 return carry
 
-            lax.fori_loop(0, PROBES, one_probe, 0)
+            lax.fori_loop(0, PROBES // 2, two_probes, 0)
 
         def force(n, carry):
             if through_node:
@@ -793,7 +798,7 @@
             pltpu.VMEM((NC, 8, LANES), F32),
             pltpu.VMEM((3 * NC, 8, LANES), F32),
             pltpu.VMEM((8, LANES), F32),
-            pltpu.VMEM((128, LANES), F32),
+            pltpu.VMEM((2, 128, LANES), F32),
             pltpu.VMEM((NC, 8, LANES), F32),
             pltpu.VMEM((8, LANES), F32),
         ]

time: 55.4 us -> 55.4 us (level)
  no operation moved by 1% of the time
where the time goes in v5:
time: 55.4 us; the launch traced here: 55.2 us
  Pallas kernels  51.8 us (94%)
  local copies, waits for them, and re-layouts  2.13 us (4%)
  between operations  1.3 us (2%)
    pallas_call x1, Pallas kernels, on_device(): pl.pallas_call(functools.partial(kernel, sizes), out_shape=(jax.ShapeDtyp...  51.8 us
    unnamed x4, local copies, waits for them, and re-layouts  2.13 us

profile of v5, /device:TPU:1, one launch (start us, length us, event | category | flops | bytes accessed | tf_op | source)
XLA Modules:
  0.0 55.2 jit_solution(11961484630805156710)
XLA Ops:
  1.3 51.8 %chebyshev.1 = (f32[192,32]{1,0:T(8,128)}, f32[4,8]{1,0:T(4,128)}) custom-call(f32[1]{0:T(128)S(6)} %copy.14.radius_ref, f32[3,4,32]{2,1,0:T(4,128)} %bitcast.9, s32[4,32]{1,0:T(4,128)} %bitcast.10, s32[128,32]{1,0:T(8,128)} %bitcast.7, f32[96,32]{1,0:T(8,128)} %bitcast.8, f32[3,128]{1,0:T(4,128)} %refs_4_.1, f32[8,64]{1,0:T(8,128)} %refs_5_.1, ...), custom_call_target="tpu_custom_call" | custom-call | tf_op jit(solution)/shard_map/chebyshev/pallas_call | solution.py:767
  53.1 0.0 copy-start
  53.1 1.5 %copy.15 = f32[2,8,3,2,2,32]{5,4,3,2,1,0:T(2,128)} copy(f32[2,8,3,2,2,32]{5,4,3,2,1,0:T(2,128)} %bitcast.6) | data formatting | bytes 49152
  54.6 0.0 copy-done
  54.6 0.6 %copy.16 = f32[4,8]{1,0:T(4,128)} copy(f32[4,8]{1,0:T(4,128)S(1)} %copy-done) | data formatting | bytes 256
Async XLA Ops:
  53.1 1.6 %copy-start = (f32[4,8]{1,0:T(4,128)S(1)}, f32[4,8]{1,0:T(4,128)}, u32[]{:S(2)}) copy-start(f32[4,8]{1,0:T(4,128)} %get-tuple-element.9) | copy-start | bytes 388
